TPU v7x, 256 devices: a whole 4x4x8 slice. The times are simulated.
256 devices in a mesh: slab: 64 (over y_hi, x, z), mp: 4 (over y_lo, core).
Axes of the slice: x: 4, y: 4 (y_hi: 2, y_lo: 2; y = y_hi * 2 + y_lo), z: 8, core: 2. Of those that a mesh axis runs over, the one named last changes fastest.
Arguments:
- query_emb: bfloat16 [16384, 1024], P('slab', 'mp'), may hold values from -6 to 6
- passage_emb: bfloat16 [32768, 1024], P('slab', 'mp'), may hold values from -6 to 6
- head: bfloat16 [1024, 1024], P('mp'), may hold values from -0.1875 to 0.1875
- fn_mask: int32 [16384, 5, 4], P('slab'), may hold values 0 or 1
- counts: int32 [64], replicated, may hold values from 1 to 512, 24576 in all
- positive_slot: int32 [16384], P('slab'), may hold values from 0 to 511
- query_weight: float32 [16384], P('slab'), may hold values from 0.5 to 2
Outputs:
- query_grad: bfloat16 [16384, 1024], P('slab', 'mp')
- passage_grad: bfloat16 [32768, 1024], P('slab', 'mp')
- head_grad: float32 [1024, 1024], P('mp')
Inputs may be any that keep to these rules, and one draw needn't show every extreme that they name: `counts`: the largest count is 512.
All inputs are finite; a program needn't handle non-finite values. No bound on the sum of `fn_mask` on one device may be relied on, other than what follows from the above.
Results may differ from a plain program's by a relative error of at most 0.034.
Values may be sent and summed in bfloat16 or wider, within the bound.
A program may use at most 64 MiB of HBM per device.

v0:
```python
import jax
import jax.numpy as jnp
from jax import lax
from jax.sharding import PartitionSpec as P

BAND = 5


EPS = 1e-06
TAU = 0.05


def shifted(value, axis, steps):
    count = lax.axis_size(axis)
    initial, last = (max(0, -steps), min(count, count - steps))
    return lax.ppermute(value, axis, [(source, source + steps) for source in range(initial, last)])


def width_sum(values):
    return lax.psum(values.astype(jnp.bfloat16), "mp").astype(jnp.float32)


def send_back(block_rows, distance):
    return shifted(block_rows.astype(jnp.bfloat16), "slab", distance).astype(block_rows.dtype)


def fetch_near(block_rows, distance):
    return shifted(block_rows, "slab", distance)


def tangent_step(unit_part, norm_part, grad_part):
    radial = jnp.sum(unit_part * grad_part, axis=1, keepdims=True)
    return ((grad_part - unit_part * radial) / norm_part).astype(jnp.bfloat16)


def body(query_emb, passage_emb, head, fn_mask, counts, positive_slot, query_weight):
    queries = query_emb.shape[0]
    passages = passage_emb.shape[0]
    mp_count = lax.axis_size("mp")
    member = lax.axis_index("mp")
    slab_index = lax.axis_index("slab")
    stacked = jnp.concatenate([query_emb, passage_emb], axis=0)
    partial_value = jnp.dot(stacked, head, preferred_element_type=jnp.float32)
    projected = lax.psum(partial_value.astype(jnp.bfloat16), "mp").astype(jnp.float32)
    row_norms = jnp.sqrt(jnp.sum(projected * projected, axis=1, keepdims=True) + EPS)
    unit_rows = projected / row_norms
    unit_half = unit_rows.astype(jnp.bfloat16)
    full_width = unit_rows.shape[1]
    padded_counts = jnp.concatenate(
        [jnp.zeros((2,), jnp.int32), counts, jnp.zeros((2,), jnp.int32)]
    )
    near_counts = lax.dynamic_slice_in_dim(padded_counts, slab_index, BAND, 0)
    query_count = queries // mp_count
    query_start = member * query_count
    own_queries = lax.dynamic_slice_in_dim(unit_half, query_start, query_count, 0)
    outgoing = unit_half[queries:]
    band_blocks = []
    for distance in (2, 1, 0, -1, -2):
        if distance == 0:
            band_blocks.append(outgoing)
        else:
            band_blocks.append(fetch_near(outgoing, distance))
    band_units = jnp.concatenate(band_blocks, axis=0)
    scores = (
        lax.dot_general(
            own_queries, band_units, (((1,), (1,)), ((), ())), preferred_element_type=jnp.float32
        )
        / TAU
    )
    scores = scores.reshape(query_count, BAND, passages)
    mask_rows = lax.dynamic_slice_in_dim(fn_mask, query_start, query_count, 0)
    tile_width = passages // fn_mask.shape[2]
    mask_cols = jnp.repeat(mask_rows, tile_width, axis=2)
    slot_ids = jnp.arange(passages, dtype=jnp.int32)
    inside = slot_ids[None, :] < near_counts[:, None]
    wanted = (
        lax.dynamic_slice_in_dim(positive_slot, query_start, query_count, 0)
        % near_counts[BAND // 2]
    )
    centre = (jnp.arange(BAND, dtype=jnp.int32) == BAND // 2)[:, None]
    is_positive = centre[None] & (slot_ids[None, None, :] == wanted[:, None, None])
    kept = inside[None] & ((mask_cols == 1) | is_positive)
    exp_terms = jnp.where(kept, jnp.exp(scores), jnp.zeros_like(scores))
    totals = jnp.sum(exp_terms, axis=(1, 2))
    weights = lax.dynamic_slice_in_dim(query_weight, query_start, query_count, 0)
    probability = exp_terms / totals[:, None, None]
    coefficient = (
        weights[:, None, None] * (probability - is_positive.astype(jnp.float32)) / TAU
    ).astype(jnp.bfloat16)
    coefficient = coefficient.reshape(query_count, BAND * passages)
    query_part = jnp.dot(coefficient, band_units, preferred_element_type=jnp.float32)
    passage_part = lax.dot_general(
        coefficient, own_queries, (((0,), (0,)), ((), ())), preferred_element_type=jnp.float32
    )
    owned = passage_part[2 * passages : 3 * passages]
    for distance in (0, 1, 3, 4):
        owned = owned + send_back(
            passage_part[distance * passages : (distance + 1) * passages], distance - 2
        )
    grads_query = lax.dynamic_update_slice_in_dim(
        jnp.zeros((queries, full_width), jnp.float32), query_part, query_start, 0
    )
    summed = width_sum(jnp.concatenate([grads_query, owned], axis=0))
    grad_proj = tangent_step(unit_rows, row_norms, summed)
    emb_grad = lax.dot_general(
        grad_proj, head, (((1,), (1,)), ((), ())), preferred_element_type=jnp.float32
    ).astype(jnp.bfloat16)
    head_part = lax.dot_general(
        stacked, grad_proj, (((0,), (0,)), ((), ())), preferred_element_type=jnp.float32
    )
    head_grad = lax.psum(head_part, "slab")
    return (emb_grad[:queries], emb_grad[queries:], head_grad)


def solution(mesh):
    return jax.shard_map(
        body,
        mesh=mesh,
        in_specs=(
            P("slab", "mp"),
            P("slab", "mp"),
            P("mp", None),
            P("slab", None, None),
            P(),
            P("slab"),
            P("slab"),
        ),
        out_specs=(P("slab", "mp"), P("slab", "mp"), P("mp", None)),
        check_vma=False,
    )
```

profile of v0, /device:TPU:8, one launch (start us, length us, event | category | flops | bytes accessed | tf_op | source)
XLA Modules:
  0.0 998.9 jit_solution(877520753371397341)
XLA Ops:
  9.2 1.7 convolution_convert_fusion
  11.1 55.8 %all-reduce.4.cloned.1.call-done = bf16[768,1024]{1,0:T(8,128)(2,1)} async-done(((bf16[768,1024]{1,0:T(8,128)(2,1)}), bf16[768,1024]{1,0:T(8,128)(2,1)}) %all-reduce.4.cloned.1.call-update) | async-done | bytes 1572880 | tf_op jit(solution)/shard_map/psum | solution.py:44
  66.9 1.8 fusion.1
  68.7 2.0 fusion.14
  71.7 5.5 collective-permute-start
  77.2 4.4 collective-permute-start.1
  83.9 1.3 collective-permute-start.2
  86.9 1.3 collective-permute-start.3
  89.4 26.5 %collective-permute-done = bf16[512,1024]{1,0:T(8,128)(2,1)} collective-permute-done((bf16[512,1024]{1,0:T(8,128)(2,1)}, bf16[512,1024]{1,0:T(8,128)(2,1)}, u32[]{:S(2)}, u32[]{:S(2)}) %collective-permute-start) | collective-permute-done | bytes 1048608 | tf_op jit(solution)/shard_map/ppermute | solution.py:16
  115.8 1.3 constant_dynamic-update-slice_fusion.6
  117.1 27.6 %collective-permute-done.1 = bf16[512,1024]{1,0:T(8,128)(2,1)} collective-permute-done((bf16[512,1024]{1,0:T(8,128)(2,1)}, bf16[512,1024]{1,0:T(8,128)(2,1)}, u32[]{:S(2)}, u32[]{:S(2)}) %collective-permute-start.1) | collective-permute-done | bytes 1048608 | tf_op jit(solution)/shard_map/ppermute | solution.py:16
  144.7 1.3 constant_dynamic-update-slice_fusion.5
  146.1 1.3 constant_dynamic-update-slice_fusion.3
  147.4 8.6 collective-permute-done.3
  156.0 1.3 constant_dynamic-update-slice_fusion.2
  157.3 1.9 select_reduce_fusion
  159.2 1.7 fusion.16
  161.3 1.3 collective-permute-start.4
  162.6 5.5 collective-permute-start.7
  168.1 1.4 collective-permute-start.6
  169.5 1.3 collective-permute-start.5
  170.9 1.3 convolution_dynamic-update-slice_fusion
  172.1 33.2 %collective-permute-done.4 = bf16[512,1024]{1,0:T(8,128)(2,1)S(1)} collective-permute-done((bf16[512,1024]{1,0:T(8,128)(2,1)S(1)}, bf16[512,1024]{1,0:T(8,128)(2,1)S(1)}, u32[]{:S(2)}, u32[]{:S(2)}) %collective-permute-start.4) | collective-permute-done | bytes 1048608 | tf_op jit(solution)/shard_map/ppermute | solution.py:16
  205.3 2.4 collective-permute-done.7
  207.7 23.3 %collective-permute-done.6 = bf16[512,1024]{1,0:T(8,128)(2,1)S(1)} collective-permute-done((bf16[512,1024]{1,0:T(8,128)(2,1)S(1)}, bf16[512,1024]{1,0:T(8,128)(2,1)S(1)}, u32[]{:S(2)}, u32[]{:S(2)}) %collective-permute-start.6) | collective-permute-done | bytes 1048608 | tf_op jit(solution)/shard_map/ppermute | solution.py:16
  232.0 1.3 pad_maximum_fusion
  233.5 55.2 %all-reduce.6.cloned.1.call-done = bf16[768,1024]{1,0:T(8,128)(2,1)} async-done(((bf16[768,1024]{1,0:T(8,128)(2,1)}), bf16[768,1024]{1,0:T(8,128)(2,1)}) %all-reduce.6.cloned.1.call-update) | async-done | bytes 1572880 | tf_op jit(solution)/shard_map/psum | solution.py:20
  288.7 2.2 fusion.2
  292.9 1.6 fusion.17
  294.5 2.0 convolution_convert_fusion.1
  297.9 692.2 %all-reduce.8.cloned.1.call-done = f32[256,1024]{1,0:T(8,128)} async-done(((f32[256,1024]{1,0:T(8,128)}), f32[256,1024]{1,0:T(8,128)}) %all-reduce.8.cloned.1.call-update) | async-done | bytes 1048592 | tf_op jit(solution)/shard_map/psum | solution.py:111
  990.1 2.3 copy.26
  (64 shorter events, 12.0 us)
Async XLA Ops:
  7.2 2.0 copy-start
  7.2 3.8 copy-start.4
  7.2 59.7 %all-reduce.4.cloned.1.call-start = ((), (), s32[]{:S(2)}) async-start(), calls=%async_computation | async-start | bytes 3145728 | tf_op jit(solution)/shard_map/psum | solution.py:44
  10.9 277.8 %all-reduce.6.cloned.1.call-start = ((), (), s32[]{:S(2)}) async-start(), calls=%async_computation.1 | async-start | bytes 3145728 | tf_op jit(solution)/shard_map/psum | solution.py:20
  11.1 70.5 %copy-start.7 = (s32[64]{0:T(128)S(1)}, s32[64]{0:T(128)}, u32[]{:S(2)}) copy-start(s32[64]{0:T(128)} %param.11) | copy-start | bytes 772
  11.1 74.0 %copy-start.5 = (s32[256]{0:T(256)S(1)}, s32[256]{0:T(256)}, u32[]{:S(2)}) copy-start(s32[256]{0:T(256)} %param.12) | copy-start | bytes 3076
  11.1 74.2 %copy-start.6 = (f32[256]{0:T(256)S(1)}, f32[256]{0:T(256)}, u32[]{:S(2)}) copy-start(f32[256]{0:T(256)} %param.13) | copy-start | bytes 3076
  71.7 44.1 %collective-permute-start = (bf16[512,1024]{1,0:T(8,128)(2,1)}, bf16[512,1024]{1,0:T(8,128)(2,1)}, u32[]{:S(2)}, u32[]{:S(2)}) collective-permute-start(bf16[512,1024]{1,0:T(8,128)(2,1)} %slice.40), channel_id=1, source_target_pairs={{0,8},{4,12},{8,16},{12,20},{16,24},{20,28},{24,32},{28,36},{32,40... | collective-permute-start | bytes 3145736 | tf_op jit(solution)/shard_map/ppermute | solution.py:16
  77.2 67.5 %collective-permute-start.1 = (bf16[512,1024]{1,0:T(8,128)(2,1)}, bf16[512,1024]{1,0:T(8,128)(2,1)}, u32[]{:S(2)}, u32[]{:S(2)}) collective-permute-start(bf16[512,1024]{1,0:T(8,128)(2,1)} %slice.40), channel_id=1, source_target_pairs={{0,4},{4,8},{8,12},{12,16},{16,20},{20,24},{24,28},{28,32},{32,36}... | collective-permute-start | bytes 3145736 | tf_op jit(solution)/shard_map/ppermute | solution.py:16
  83.9 62.2 %collective-permute-start.2 = (bf16[512,1024]{1,0:T(8,128)(2,1)}, bf16[512,1024]{1,0:T(8,128)(2,1)}, u32[]{:S(2)}, u32[]{:S(2)}) collective-permute-start(bf16[512,1024]{1,0:T(8,128)(2,1)} %slice.40), channel_id=1, source_target_pairs={{4,0},{8,4},{12,8},{16,12},{20,16},{24,20},{28,24},{32,28},{36,32}... | collective-permute-start | bytes 3145736 | tf_op jit(solution)/shard_map/ppermute | solution.py:16
  86.9 69.1 %collective-permute-start.3 = (bf16[512,1024]{1,0:T(8,128)(2,1)}, bf16[512,1024]{1,0:T(8,128)(2,1)}, u32[]{:S(2)}, u32[]{:S(2)}) collective-permute-start(bf16[512,1024]{1,0:T(8,128)(2,1)} %slice.40), channel_id=1, source_target_pairs={{8,0},{12,4},{16,8},{20,12},{24,16},{28,20},{32,24},{36,28},{40,32... | collective-permute-start | bytes 3145736 | tf_op jit(solution)/shard_map/ppermute | solution.py:16
  161.3 44.0 %collective-permute-start.4 = (bf16[512,1024]{1,0:T(8,128)(2,1)S(1)}, bf16[512,1024]{1,0:T(8,128)(2,1)S(1)}, u32[]{:S(2)}, u32[]{:S(2)}) collective-permute-start(bf16[512,1024]{1,0:T(8,128)(2,1)S(1)} %get-tuple-element.3), channel_id=1, source_target_pairs={{8,0},{12,4},{16,8},{20,12},{24,16},{28,20},{32,24},{36,28},{40,32... | collective-permute-start | bytes 3145736 | tf_op jit(solution)/shard_map/ppermute | solution.py:16
  162.6 45.1 %collective-permute-start.7 = (bf16[512,1024]{1,0:T(8,128)(2,1)S(1)}, bf16[512,1024]{1,0:T(8,128)(2,1)S(1)}, u32[]{:S(2)}, u32[]{:S(2)}) collective-permute-start(bf16[512,1024]{1,0:T(8,128)(2,1)S(1)} %get-tuple-element.4), channel_id=1, source_target_pairs={{0,8},{4,12},{8,16},{12,20},{16,24},{20,28},{24,32},{28,36},{32,40... | collective-permute-start | bytes 3145736 | tf_op jit(solution)/shard_map/ppermute | solution.py:16
  168.1 62.8 %collective-permute-start.6 = (bf16[512,1024]{1,0:T(8,128)(2,1)S(1)}, bf16[512,1024]{1,0:T(8,128)(2,1)S(1)}, u32[]{:S(2)}, u32[]{:S(2)}) collective-permute-start(bf16[512,1024]{1,0:T(8,128)(2,1)S(1)} %get-tuple-element.5), channel_id=1, source_target_pairs={{0,4},{4,8},{8,12},{12,16},{16,20},{20,24},{24,28},{28,32},{32,36}... | collective-permute-start | bytes 3145736 | tf_op jit(solution)/shard_map/ppermute | solution.py:16
  169.5 61.5 %collective-permute-start.5 = (bf16[512,1024]{1,0:T(8,128)(2,1)S(1)}, bf16[512,1024]{1,0:T(8,128)(2,1)S(1)}, u32[]{:S(2)}, u32[]{:S(2)}) collective-permute-start(bf16[512,1024]{1,0:T(8,128)(2,1)S(1)} %get-tuple-element.6), channel_id=1, source_target_pairs={{4,0},{8,4},{12,8},{16,12},{20,16},{24,20},{28,24},{32,28},{36,32}... | collective-permute-start | bytes 3145736 | tf_op jit(solution)/shard_map/ppermute | solution.py:16
  232.0 56.8 %copy-start.1 = (bf16[768,1024]{1,0:T(8,128)(2,1)S(1)}, bf16[768,1024]{1,0:T(8,128)(2,1)}, u32[]{:S(2)}) copy-start(bf16[768,1024]{1,0:T(8,128)(2,1)} %all-reduce.4.cloned.1.call-done) | copy-start | bytes 4718596
  233.3 756.8 %all-reduce.8.cloned.1.call-start = ((), (), s32[]{:S(2)}) async-start(), calls=%async_computation.2 | async-start | bytes 2097152 | tf_op jit(solution)/shard_map/psum | solution.py:111
  288.7 2.2 copy-start.3
  291.7 1.1 copy-start.2
Sparse Core Ops, SparseCore 0:
  11.1 55.8 all-reduce.3
  233.4 55.2 all-reduce.5
  294.6 695.4 all-reduce.7
where the time goes:
time: 1000 us; the launch traced here: 999 us
  waiting for transfers between devices  925 us (92%)
  starting transfers between devices  22.2 us (2%)
  local copies, waits for them, and re-layouts  16.7 us (2%)
  between operations  15.4 us (2%)
  matrix products  10.1 us (1%)
    psum x1, waiting for transfers between devices, body(): head_grad = lax.psum(head_part, 'slab')  692 us
    ppermute x8, waiting for transfers between devices, shifted(): lax.ppermute(value, axis, [(source, source + steps) for source in range(i...  122 us
    psum x1, waiting for transfers between devices, body(): lax.psum(partial_value.astype(jnp.bfloat16), 'mp').astype(jnp.float32)  55.8 us
    psum x1, waiting for transfers between devices, width_sum(): return lax.psum(values.astype(jnp.bfloat16), 'mp').astype(jnp.float32)  55.2 us
    ppermute x8, starting transfers between devices, shifted(): lax.ppermute(value, axis, [(source, source + steps) for source in range(i...  21.9 us
  transfers between devices with their start and end apart: 11, of which 9 were waited for; matrix products, arithmetic and copies ran while one was open for 1% of the time, Pallas kernels for 0%

commit v1 on v0

v1 whole, which is shorter than its diff:
```python
import jax
import jax.numpy as jnp
from jax import lax
from jax.experimental import pallas as pl
from jax.experimental.pallas import tpu as pltpu
from jax.sharding import PartitionSpec as P

EPS = 1e-06
TAU = 0.05
D = 1024
QM = 64
PM = 128
NQ = 5 * QM
SEMS = 96
MESH = pl.DeviceIdType.MESH
BF = jnp.bfloat16
F32 = jnp.float32


def kernel(
    q_ref, p_ref, head_ref, mask_ref, counts_ref, pos_ref, weight_ref,
    oq_ref, op_ref, oh_ref,
    part_q, part_p, rq, rp, yq, yp, zq, zp,
    unit_q, unit_p, norm_q, norm_p,
    qb, pb, auxs, auxr, auxc, ef, eb, tts, ttr, gs, gr,
    pps, ppf, pr, py, pz, pgq, pgp,
    hf, hb, ax, bz, a1, b1, az, bx, a1f, b1f, c2, cr, ga, gb, gaf, gbf,
    ssem, rsem,
):
    slab = lax.axis_index("slab")
    m = lax.axis_index("mp")
    core, low = m % 2, m // 2
    sib = 2 * low + 1 - core
    opp = 2 * (1 - low) + core
    osib = 2 * (1 - low) + 1 - core
    high, xi, zi = slab // 32, (slab // 8) % 4, slab % 8

    def at_slab(distance):
        return ((slab + distance + 64) % 64, m)

    def at_x(step):
        return (high * 32 + ((xi + step) % 4) * 8 + zi, m)

    def at_z(step):
        return (high * 32 + xi * 8 + (zi + step) % 8, m)

    to_sib, to_opp, to_high = (slab, sib), (slab, opp), ((slab + 32) % 64, m)
    peers = [to_sib, to_opp, to_high]
    peers += [at_slab(k) for k in (-4, -3, -2, -1, 1, 2, 3, 4)]
    peers += [at_x(k) for k in range(1, 4)] + [at_z(k) for k in range(1, 8)]
    used = [0]

    def send(src, dst, device):
        i = used[0]
        used[0] += 1
        copy = pltpu.make_async_remote_copy(
            src_ref=src, dst_ref=dst, send_sem=ssem.at[i], recv_sem=rsem.at[i],
            device_id=device, device_id_type=MESH,
        )
        copy.start()
        sent.append(copy)
        return copy

    sent = []

    def rows(count, index):
        return pl.ds(pl.multiple_of(count * index, count), count)

    barrier = pltpu.get_barrier_semaphore()
    for peer in peers:
        pl.semaphore_signal(barrier, inc=1, device_id=peer, device_id_type=MESH)

    part_q[...] = jnp.dot(q_ref[...], head_ref[...], preferred_element_type=F32).astype(BF)
    pl.semaphore_wait(barrier, len(peers))
    q1 = send(part_q.at[rows(QM, osib)], rq.at[1], to_sib)
    q0 = send(part_q.at[rows(QM, sib)], rq.at[0], to_sib)
    part_p[...] = jnp.dot(p_ref[...], head_ref[...], preferred_element_type=F32).astype(BF)
    p1 = send(part_p.at[rows(PM, osib)], rp.at[1], to_sib)
    p0 = send(part_p.at[rows(PM, sib)], rp.at[0], to_sib)
    q1.wait_recv()
    yq[...] = (part_q[rows(QM, opp)].astype(F32) + rq[1].astype(F32)).astype(BF)
    q2 = send(yq, zq, to_opp)
    p1.wait_recv()
    yp[...] = (part_p[rows(PM, opp)].astype(F32) + rp[1].astype(F32)).astype(BF)
    p2 = send(yp, zp, to_opp)

    def own_lanes(value):
        quarters = [value[:, k * QM : (k + 1) * QM] for k in range(4)]
        return jnp.where(
            m == 0, quarters[0],
            jnp.where(m == 1, quarters[1], jnp.where(m == 2, quarters[2], quarters[3])),
        )

    count = counts_ref[slab]
    count_f = count.astype(F32)
    weight = own_lanes(weight_ref[...])
    slot = own_lanes(pos_ref[...].astype(F32))
    wanted = slot - count_f * jnp.floor((slot + 0.5) / count_f)
    auxs[...] = jnp.zeros_like(auxs)
    for k in range(5):
        auxs[k, 0:4, 0:QM] = own_lanes(mask_ref[k].astype(F32))
        auxs[k, 4:5, 0:QM] = weight

    def normalise(projected):
        norm = jnp.sqrt(jnp.sum(projected * projected, axis=1, keepdims=True) + EPS)
        return projected / norm, norm

    q0.wait_recv()
    q2.wait_recv()
    unit, norm = normalise(
        part_q[rows(QM, m)].astype(F32) + rq[0].astype(F32) + zq[...].astype(F32)
    )
    unit_q[...] = unit
    norm_q[...] = norm
    qb[2 * QM : 3 * QM] = unit.astype(BF)
    queries, auxes = [], []
    for k in (1, -1, 2, -2):
        queries.append(
            send(qb.at[2 * QM : 3 * QM], qb.at[(2 - k) * QM : (3 - k) * QM], at_slab(k))
        )
        auxes.append(send(auxs.at[2 + k], auxr.at[2 - k], at_slab(k)))

    p0.wait_recv()
    p2.wait_recv()
    unit, norm = normalise(
        part_p[rows(PM, m)].astype(F32) + rp[0].astype(F32) + zp[...].astype(F32)
    )
    unit_p[...] = unit
    norm_p[...] = norm
    pb[rows(PM, m)] = unit.astype(BF)

    def gather(ref, size):
        mine = ref.at[rows(size, m)]
        over = send(mine, mine, to_opp)
        near = send(mine, mine, to_sib)
        over.wait_recv()
        theirs = ref.at[rows(size, opp)]
        far = send(theirs, theirs, to_sib)
        near.wait_recv()
        far.wait_recv()

    gather(pb, PM)
    for copy in queries + auxes:
        copy.wait_recv()

    auxr[2] = auxs[2]
    for k in range(5):
        auxc[:, k * QM : (k + 1) * QM] = auxr[k][:, 0:QM]
        here = slab + (k - 2)
        real = jnp.where(here >= 0, jnp.where(here < 64, 1.0, 0.0), 0.0).astype(F32)
        auxc[0:4, k * QM : (k + 1) * QM] = auxr[k][0:4, 0:QM] * real
        auxc[5:6, k * QM : (k + 1) * QM] = wanted if k == 2 else jnp.full((1, QM), -1.0, F32)
    scores = lax.dot_general(
        pb[...], qb[...], (((1,), (1,)), ((), ())), preferred_element_type=F32
    )
    slot_ids = lax.broadcasted_iota(jnp.int32, (PM, NQ), 0)
    others = jnp.zeros((1, NQ), F32)
    positive = jnp.zeros((1, NQ), F32)
    for tile in range(4):
        ids = slot_ids + tile * PM
        is_positive = ids.astype(F32) == auxc[5:6, :]
        kept = (ids < count) & (auxc[tile : tile + 1, :] > 0.5) & jnp.logical_not(is_positive)
        grown = jnp.exp(scores[tile * PM : (tile + 1) * PM] / TAU)
        terms = jnp.where(kept, grown, 0.0)
        others = others + jnp.sum(terms, axis=0, keepdims=True)
        positive = positive + jnp.sum(jnp.where(is_positive, grown, 0.0), axis=0, keepdims=True)
        ef[tile * PM : (tile + 1) * PM] = terms
        eb[tile * PM : (tile + 1) * PM] = terms.astype(BF)
    tts[...] = jnp.zeros_like(tts)
    tts[0:1, 0:NQ] = others
    tts[1:2, 0:NQ] = positive
    totals = [send(tts, ttr.at[4 - k], at_slab(k)) for k in (1, -1, 2, -2, 3, -3, 4, -4)]

    terms = lax.dot_general(
        eb[...], pb[...], (((0,), (0,)), ((), ())), preferred_element_type=F32
    )
    returns = []
    for k in (2, -2, 1, -1):
        gs[2 + k] = terms[(2 + k) * QM : (3 + k) * QM].astype(BF)
        returns.append(send(gs.at[2 + k], gr.at[2 - k], at_slab(k)))
    own_terms = terms[2 * QM : 3 * QM]

    ttr[4] = tts[...]
    for copy in totals:
        copy.wait_recv()
    for k in range(-2, 3):
        rest = jnp.zeros((1, QM), F32)
        for j in range(-2, 3):
            rest = rest + ttr[k + j + 4][0:1, (2 - j) * QM : (3 - j) * QM]
        whole = rest + ttr[k + 4][1:2, 2 * QM : 3 * QM]
        lanes = slice((2 + k) * QM, (3 + k) * QM)
        auxc[6:7, lanes] = auxc[4:5, lanes] / (whole * TAU)
        if k == 0:
            own_rest, own_whole = rest, whole
            auxc[7:8, lanes] = auxc[6:7, lanes] * rest
        else:
            auxc[7:8, lanes] = jnp.zeros((1, QM), F32)

    for tile in range(4):
        here = slice(tile * PM, (tile + 1) * PM)
        is_positive = (slot_ids + tile * PM).astype(F32) == auxc[5:6, :]
        coefficient = jnp.where(is_positive, -auxc[7:8, :], ef[here] * auxc[6:7, :])
        part = jnp.dot(coefficient.astype(BF), qb[...], preferred_element_type=F32)
        ppf[here] = part
        pps[here] = part.astype(BF)
    p1 = send(pps.at[rows(PM, osib)], pr.at[1], to_sib)
    p0 = send(pps.at[rows(PM, sib)], pr.at[0], to_sib)
    p1.wait_recv()
    py[...] = (ppf[rows(PM, opp)] + pr[1].astype(F32)).astype(BF)
    p2 = send(py, pz, to_opp)

    def tangent(unit, norm, grad):
        radial = jnp.sum(unit * grad, axis=1, keepdims=True)
        return ((grad - unit * radial) / norm).astype(BF)

    eye = lax.broadcasted_iota(jnp.int32, (QM, QM), 0) == lax.broadcasted_iota(
        jnp.int32, (QM, QM), 1
    )

    def column(row):
        return jnp.sum(jnp.where(eye, row, 0.0), axis=1, keepdims=True)

    one_hot = (
        lax.broadcasted_iota(jnp.int32, (4 * PM, QM), 0).astype(F32) == wanted
    ).astype(F32).astype(BF)
    chosen = lax.dot_general(
        one_hot, pb[...], (((0,), (0,)), ((), ())), preferred_element_type=F32
    )
    scale = column(weight / (own_whole * TAU))
    drop = column(weight * own_rest / (own_whole * TAU))
    for copy in returns:
        copy.wait_recv()
    for k in (0, 1, 3, 4):
        own_terms = own_terms + gr[k].astype(F32)
    pgq[rows(QM, m)] = tangent(unit_q[...], norm_q[...], own_terms * scale - chosen * drop)
    gather(pgq, QM)
    p0.wait_recv()
    p2.wait_recv()
    summed = ppf[rows(PM, m)] + pr[0].astype(F32) + pz[...].astype(F32)
    pgp[rows(PM, m)] = tangent(unit_p[...], norm_p[...], summed)
    gather(pgp, PM)

    across = (((0,), (0,)), ((), ()))
    term = lax.dot_general(
        q_ref[...], pgq[...], across, preferred_element_type=F32
    ) + lax.dot_general(p_ref[...], pgp[...], across, preferred_element_type=F32)
    hf[...] = term
    hb[...] = term.astype(BF)

    def cols(index):
        return pl.ds(pl.multiple_of(index * 128, 128), 128)

    first = []
    for k in (2, 1, 3):
        first.append(send(hb.at[rows(48, (xi + k) % 4)], ax.at[k - 1], at_x(k)))
    for k in (4, 3, 5, 2, 6, 1, 7):
        first.append(send(hb.at[192:256, cols((zi + k) % 8)], bz.at[k - 1], at_z(k)))

    back = (((1,), (1,)), ((), ()))
    oq_ref[...] = lax.dot_general(
        pgq[...], head_ref[...], back, preferred_element_type=F32
    ).astype(BF)
    op_ref[...] = lax.dot_general(
        pgp[...], head_ref[...], back, preferred_element_type=F32
    ).astype(BF)

    for copy in first:
        copy.wait_recv()
    total = hf[rows(48, xi)]
    for k in range(3):
        total = total + ax[k].astype(F32)
    a1f[...] = total
    a1[...] = total.astype(BF)
    total = hf[192:256, cols(zi)]
    for k in range(7):
        total = total + bz[k].astype(F32)
    b1f[...] = total
    b1[...] = total.astype(BF)
    second = []
    for k in (4, 3, 5, 2, 6, 1, 7):
        second.append(send(a1.at[:, cols((zi + k) % 8)], az.at[k - 1], at_z(k)))
    for k in (2, 1, 3):
        second.append(send(b1.at[rows(16, (xi + k) % 4)], bx.at[k - 1], at_x(k)))
    for copy in second:
        copy.wait_recv()
    total = a1f[:, cols(zi)]
    for k in range(7):
        total = total + az[k].astype(F32)
    c2[0:48] = total.astype(BF)
    total = b1f[rows(16, xi)]
    for k in range(3):
        total = total + bx[k].astype(F32)
    c2[48:64] = total.astype(BF)
    send(c2, cr, to_high).wait_recv()
    final = (c2[...].astype(F32) + cr[...].astype(F32)).astype(BF)
    ga[:, cols(zi)] = final[0:48]
    gb[rows(16, xi)] = final[48:64]
    third = []
    for k in (4, 3, 5, 2, 6, 1, 7):
        third.append(send(ga.at[:, cols(zi)], ga.at[:, cols(zi)], at_z(k)))
    fourth = []
    for k in (2, 1, 3):
        fourth.append(send(gb.at[rows(16, xi)], gb.at[rows(16, xi)], at_x(k)))
    for copy in fourth:
        copy.wait_recv()
    last = []
    for k in (4, 3, 5, 2, 6, 1, 7):
        last.append(send(gb, gbf.at[:, cols(zi)], at_z(k)))
    for copy in third:
        copy.wait_recv()
    for k in (2, 1, 3):
        last.append(send(ga, gaf.at[rows(48, xi)], at_x(k)))
    gaf[rows(48, xi)] = ga[...]
    gbf[:, cols(zi)] = gb[...]
    for copy in last:
        copy.wait_recv()
    oh_ref[0:192] = gaf[...].astype(F32)
    oh_ref[192:256] = gbf[...].astype(F32)
    for copy in sent:
        copy.wait_send()


def body(query_emb, passage_emb, head, fn_mask, counts, positive_slot, query_weight):
    vmem = pl.BlockSpec(memory_space=pltpu.VMEM)
    smem = pl.BlockSpec(memory_space=pltpu.SMEM)

    def half(*shape):
        return pltpu.VMEM(shape, BF)

    def full(*shape):
        return pltpu.VMEM(shape, F32)

    return pl.pallas_call(
        kernel,
        out_shape=(
            jax.ShapeDtypeStruct((256, 256), BF),
            jax.ShapeDtypeStruct((512, 256), BF),
            jax.ShapeDtypeStruct((256, D), F32),
        ),
        in_specs=[vmem, vmem, vmem, vmem, smem, vmem, vmem],
        out_specs=(vmem, vmem, vmem),
        scratch_shapes=[
            half(256, D), half(512, D), half(2, QM, D), half(2, PM, D),
            half(QM, D), half(PM, D), half(QM, D), half(PM, D),
            full(QM, D), full(PM, D), full(QM, 1), full(PM, 1),
            half(NQ, D), half(4 * PM, D), full(5, 8, 128), full(5, 8, 128), full(8, NQ),
            full(4 * PM, NQ), half(4 * PM, NQ), full(8, 384), full(9, 8, 384),
            half(5, QM, D), half(5, QM, D),
            half(512, D), full(512, D), half(2, PM, D), half(PM, D), half(PM, D),
            half(256, D), half(512, D),
            full(256, D), half(256, D), half(3, 48, D), half(7, 64, 128),
            half(48, D), half(64, 128), half(7, 48, 128), half(3, 16, 128),
            full(48, D), full(64, 128), half(64, 128), half(64, 128),
            half(48, D), half(64, 128), half(192, D), half(64, D),
            pltpu.SemaphoreType.DMA((SEMS,)), pltpu.SemaphoreType.DMA((SEMS,)),
        ],
        compiler_params=pltpu.CompilerParams(
            collective_id=0, has_side_effects=True, vmem_limit_bytes=48 << 20
        ),
        cost_estimate=pl.CostEstimate(flops=3 << 30, bytes_accessed=4 << 20, transcendentals=0),
    )(
        query_emb, passage_emb, head, jnp.transpose(fn_mask, (1, 2, 0)), counts,
        positive_slot.reshape(1, -1), query_weight.reshape(1, -1),
    )


def solution(mesh):
    return jax.shard_map(
        body,
        mesh=mesh,
        in_specs=(
            P("slab", "mp"), P("slab", "mp"), P("mp", None), P("slab", None, None),
            P(), P("slab"), P("slab"),
        ),
        out_specs=(P("slab", "mp"), P("slab", "mp"), P("mp", None)),
        check_vma=False,
    )
```

time: 1000 us -> 104 us (0.10)
  waiting for transfers between devices: 925 us -> 0 us
  Pallas kernels: 0 us -> 96.3 us
  starting transfers between devices: 22.2 us -> 0 us
  between operations: 15.4 us -> 0.67 us
  matrix products: 10.1 us -> 0 us
  local copies, waits for them, and re-layouts: 16.7 us -> 6.62 us
    psum x3 -> x0, waiting for transfers between devices: 803 us -> none  [the longest x1 692 us: body(): head_grad = lax.psum(head_part, 'slab')]
    ppermute x8 -> x0, waiting for transfers between devices: 122 us -> none  [shifted(): lax.ppermute(value, axis, [(source, source + steps) for source in range(i...]
    pallas_call x0 -> x1, Pallas kernels: none -> 96.3 us  [body(): pl.pallas_call(kernel, out_shape=(jax.ShapeDtypeStruct((256, 256), BF), j...]
    ppermute x8 -> x0, starting transfers between devices: 21.9 us -> none  [shifted(): lax.ppermute(value, axis, [(source, source + steps) for source in range(i...]
    dot_general x6 -> x0, matrix products: 10.1 us -> none  [the longest x1 2.02 us: body(): lax.dot_general(grad_proj, head, (((1,), (1,)), ((), ())), preferred_elem...]
  transfers between devices with their start and end apart: 11 -> 0, of which waited for: 9 -> 0; matrix products, arithmetic and copies ran while one was open for 1% -> 0% of each run, Pallas kernels for 0% -> 0%
where the time goes in v1:
time: 104 us
  Pallas kernels  96.3 us (93%)
  local copies, waits for them, and re-layouts  6.62 us (6%)
    pallas_call x1, Pallas kernels, body(): pl.pallas_call(kernel, out_shape=(jax.ShapeDtypeStruct((256, 256), BF), j...  96.3 us
    unnamed x17, local copies, waits for them, and re-layouts  6.62 us

profile of v1, /device:TPU:8, one launch (start us, length us, event | category | flops | bytes accessed | tf_op | source)
XLA Modules:
  0.0 103.6 jit_solution(16810504527091000057)
XLA Ops:
  0.6 0.0 copy-start.5
  0.6 0.0 copy-start.4
  0.7 0.0 copy-start.6
  0.7 0.7 copy-done.5
  1.3 0.0 copy-done.4
  1.3 0.0 copy-done.6
  1.3 0.0 copy-start
  1.3 1.0 %copy-done = bf16[256,1024]{1,0:T(8,128)(2,1)S(1)} copy-done((bf16[256,1024]{1,0:T(8,128)(2,1)S(1)}, bf16[256,1024]{1,0:T(8,128)(2,1)}, u32[]{:S(2)}) %copy-start) | copy-done | bytes 524312
  2.4 0.0 copy-start.1
  2.4 0.9 copy-done.1
  3.3 0.0 copy-start.2
  3.3 0.9 copy-done.2
  4.2 0.0 copy-start.3
  4.2 0.7 copy-done.3
  5.0 96.3 %shard_map.94 = (bf16[256,256]{1,0:T(8,128)(2,1)S(1)}, bf16[512,256]{1,0:T(8,128)(2,1)S(1)}, f32[256,1024]{1,0:T(8,128)S(1)}) custom-call(bf16[256,256]{1,0:T(8,128)(2,1)S(1)} %copy-done.2, bf16[512,256]{1,0:T(8,128)(2,1)S(1)} %copy-done.1, bf16[256,1024]{1,0:T(8,128)(2,1)S(1)} %copy-done, s32[5,4,256]{2,1,0:T(4,128)S(1)} %bitcast.3, s32[64]{0:T(128)S(1)} %copy-done.6, ...), custom_call_target="tpu_custom_call" | custom-call | flops 3221225472 | bytes 4194304 | tf_op jit(solution)/shard_map/pallas_call | solution.py:333
  101.3 0.7 copy.13
  101.9 0.7 copy.14
  102.6 1.0 copy.15
Async XLA Ops:
  0.6 0.7 copy-start.5
  0.6 0.7 copy-start.4
  0.7 0.7 copy-start.6
  1.3 1.0 %copy-start = (bf16[256,1024]{1,0:T(8,128)(2,1)S(1)}, bf16[256,1024]{1,0:T(8,128)(2,1)}, u32[]{:S(2)}) copy-start(bf16[256,1024]{1,0:T(8,128)(2,1)} %head_ref.1) | copy-start | bytes 1572868
  2.4 0.9 copy-start.1
  3.3 0.9 copy-start.2
  4.2 0.7 copy-start.3

commit v2 on v1

v2 whole, which is shorter than its diff:
```python
import jax
import jax.numpy as jnp
from jax import lax
from jax.experimental import pallas as pl
from jax.experimental.pallas import tpu as pltpu
from jax.sharding import PartitionSpec as P

EPS = 1e-06
TAU = 0.05
D = 1024
QM = 64
PM = 128
NQ = 5 * QM
SEMS = 112
MESH = pl.DeviceIdType.MESH
BF = jnp.bfloat16
F32 = jnp.float32


def kernel(
    q_hbm, p_hbm, head_hbm, mask_hbm, counts_ref, pos_hbm, weight_hbm,
    oq_ref, op_ref, oh_ref,
    q_ref, p_ref, head, mask_ref, pos_ref, weight_ref,
    part_q, part_p, rq, rp, yq, yp, zq, zp,
    unit_q, unit_p, norm_q, norm_p,
    qb, pb, auxs, auxr, auxc, ef, eb, tts, ttr, gs, gr,
    pps, ppf, pr, py, pz, xo, pgo, eo,
    tsend, trecv, hf, hb, ax, cy, a1f, c1f, a1, c1, ay, cx, e1f, e1, ez, gz,
    lsem, ssem, rsem,
):
    slab = lax.axis_index("slab")
    m = lax.axis_index("mp")
    core, low = m % 2, m // 2
    sib = 2 * low + 1 - core
    opp = 2 * (1 - low) + core
    osib = 2 * (1 - low) + 1 - core
    high, xi, zi = slab // 32, (slab // 8) % 4, slab % 8

    def at_slab(distance):
        there = (slab + distance + 64) % 64
        return (there, jnp.where(there // 32 == high, m, opp))

    def at_x(step):
        return (high * 32 + ((xi + step) % 4) * 8 + zi, m)

    def at_z(step):
        return (high * 32 + xi * 8 + (zi + step) % 8, m)

    def inside(distance):
        return jnp.logical_and(slab + distance >= 0, slab + distance < 64)

    to_sib, to_opp, to_osib = (slab, sib), (slab, opp), (slab, osib)
    to_high, to_back = ((slab + 32) % 64, m), ((slab + 32) % 64, opp)
    peers = [to_sib, to_opp, to_osib, to_high, to_back]
    peers += [at_slab(k) for k in (-4, -3, -2, -1, 1, 2, 3, 4)]
    peers += [at_x(k) for k in range(1, 4)] + [at_z(k) for k in range(1, 8)]
    sent = []

    class Send:
        def __init__(self, src, dst, device, leaves=None, comes=None):
            i = len(sent)
            self.copy = pltpu.make_async_remote_copy(
                src_ref=src, dst_ref=dst, send_sem=ssem.at[i], recv_sem=rsem.at[i],
                device_id=device, device_id_type=MESH,
            )
            self.leaves, self.comes = leaves, comes
            self.act(leaves, self.copy.start)
            sent.append(self)

        def act(self, condition, action):
            if condition is None:
                action()
            else:
                pl.when(condition)(action)

        def wait_recv(self):
            self.act(self.comes, self.copy.wait_recv)

        def wait_send(self):
            self.act(self.leaves, self.copy.wait_send)

    def near_slab(src, dst, distance):
        return Send(src, dst, at_slab(distance), inside(distance), inside(-distance))

    def rows(count, index):
        return pl.ds(pl.multiple_of(count * index, count), count)

    barrier = pltpu.get_barrier_semaphore()
    for peer in peers:
        pl.semaphore_signal(barrier, inc=1, device_id=peer, device_id_type=MESH)
    loads = [
        pltpu.make_async_copy(src, dst, lsem.at[i])
        for i, (src, dst) in enumerate((
            (q_hbm, q_ref), (head_hbm, head.at[rows(256, m)]), (p_hbm, p_ref),
            (mask_hbm, mask_ref), (pos_hbm, pos_ref), (weight_hbm, weight_ref),
        ))
    ]
    for copy in loads:
        copy.start()

    for k in (-4, -3, -2, -1, 1, 2, 3, 4):
        @pl.when(jnp.logical_not(inside(k)))
        def _():
            ttr[k + 4] = jnp.zeros((4, 128), F32)
            if abs(k) <= 2:
                qb[(2 + k) * QM : (3 + k) * QM] = jnp.zeros((QM, D), BF)
                gr[k + 2] = jnp.zeros((QM, D), BF)
                auxr[k + 2] = jnp.zeros((8, 128), F32)

    loads[0].wait()
    loads[1].wait()
    own_head = head[rows(256, m)]
    part_q[...] = jnp.dot(q_ref[...], own_head, preferred_element_type=F32).astype(BF)
    pl.semaphore_wait(barrier, len(peers))
    q1 = Send(part_q.at[rows(QM, osib)], rq.at[1], to_sib)
    q0 = Send(part_q.at[rows(QM, sib)], rq.at[0], to_sib)
    mine = head.at[rows(256, m)]
    heads = [Send(mine, mine, to_back)]
    loads[2].wait()
    part_p[...] = jnp.dot(p_ref[...], own_head, preferred_element_type=F32).astype(BF)
    p1 = Send(part_p.at[rows(PM, osib)], rp.at[1], to_sib)
    p0 = Send(part_p.at[rows(PM, sib)], rp.at[0], to_sib)
    q1.wait_recv()
    yq[...] = (part_q[rows(QM, opp)].astype(F32) + rq[1].astype(F32)).astype(BF)
    q2 = Send(yq, zq, to_opp)
    p1.wait_recv()
    yp[...] = (part_p[rows(PM, opp)].astype(F32) + rp[1].astype(F32)).astype(BF)
    p2 = Send(yp, zp, to_opp)

    def own_lanes(value):
        quarters = [value[:, k * QM : (k + 1) * QM] for k in range(4)]
        return jnp.where(
            m == 0, quarters[0],
            jnp.where(m == 1, quarters[1], jnp.where(m == 2, quarters[2], quarters[3])),
        )

    for copy in loads[3:]:
        copy.wait()
    count = counts_ref[slab]
    count_f = count.astype(F32)
    weight = own_lanes(weight_ref[...])
    slot = own_lanes(pos_ref[...].astype(F32))
    wanted = slot - count_f * jnp.floor((slot + 0.5) / count_f)
    auxs[...] = jnp.zeros_like(auxs)
    for k in range(5):
        auxs[k, 0:4, 0:QM] = own_lanes(mask_ref[k].astype(F32))
        auxs[k, 4:5, 0:QM] = weight
    xo[0:QM, rows(256, m)] = q_ref[rows(QM, m)]
    xo[QM:, rows(256, m)] = p_ref[rows(PM, m)]

    def normalise(projected):
        norm = jnp.sqrt(jnp.sum(projected * projected, axis=1, keepdims=True) + EPS)
        return projected / norm, norm

    q0.wait_recv()
    q2.wait_recv()
    unit, norm = normalise(
        part_q[rows(QM, m)].astype(F32) + rq[0].astype(F32) + zq[...].astype(F32)
    )
    unit_q[...] = unit
    norm_q[...] = norm
    qb[2 * QM : 3 * QM] = unit.astype(BF)
    queries, auxes = [], []
    for k in (1, -1, 2, -2):
        queries.append(
            near_slab(qb.at[2 * QM : 3 * QM], qb.at[(2 - k) * QM : (3 - k) * QM], k)
        )
        auxes.append(near_slab(auxs.at[2 + k], auxr.at[2 - k], k))

    p0.wait_recv()
    p2.wait_recv()
    unit, norm = normalise(
        part_p[rows(PM, m)].astype(F32) + rp[0].astype(F32) + zp[...].astype(F32)
    )
    unit_p[...] = unit
    norm_p[...] = norm
    pb[rows(PM, m)] = unit.astype(BF)

    def piece(member, part):
        return pb.at[pl.ds(pl.multiple_of(member * PM + part * 64, 64), 64)]

    over = [Send(piece(m, h), piece(m, h), to_opp) for h in range(2)]
    near = Send(pb.at[rows(PM, m)], pb.at[rows(PM, m)], to_sib)
    wide = []
    for member, device in ((opp, to_opp), (osib, to_osib), (sib, to_sib)):
        wide.append(
            Send(q_ref.at[rows(QM, member)], xo.at[0:QM, rows(256, m)], device)
        )
        wide.append(
            Send(p_ref.at[rows(PM, member)], xo.at[QM : QM + PM, rows(256, m)], device)
        )
    far = []
    for h in range(2):
        over[h].wait_recv()
        far.append(Send(piece(opp, h), piece(opp, h), to_sib))
    heads.append(Send(mine, mine, to_sib))
    for copy in [near] + far:
        copy.wait_recv()
    for copy in queries + auxes:
        copy.wait_recv()

    auxr[2] = auxs[2]
    for k in range(5):
        lanes = slice(k * QM, (k + 1) * QM)
        auxc[:, lanes] = auxr[k][:, 0:QM]
        auxc[5:6, lanes] = wanted if k == 2 else jnp.full((1, QM), -1.0, F32)
    scores = lax.dot_general(
        pb[...], qb[...], (((1,), (1,)), ((), ())), preferred_element_type=F32
    )
    slot_ids = lax.broadcasted_iota(jnp.int32, (PM, NQ), 0)
    others = jnp.zeros((1, NQ), F32)
    positive = jnp.zeros((1, NQ), F32)
    for tile in range(4):
        ids = slot_ids + tile * PM
        is_positive = ids.astype(F32) == auxc[5:6, :]
        kept = (ids < count) & (auxc[tile : tile + 1, :] > 0.5) & jnp.logical_not(is_positive)
        grown = jnp.exp(scores[tile * PM : (tile + 1) * PM] / TAU)
        terms = jnp.where(kept, grown, 0.0)
        others = others + jnp.sum(terms, axis=0, keepdims=True)
        positive = positive + jnp.sum(jnp.where(is_positive, grown, 0.0), axis=0, keepdims=True)
        ef[tile * PM : (tile + 1) * PM] = terms
        eb[tile * PM : (tile + 1) * PM] = terms.astype(BF)
    for k in range(5):
        tts[k // 2 : k // 2 + 1, (k % 2) * QM : (k % 2 + 1) * QM] = others[
            :, k * QM : (k + 1) * QM
        ]
    tts[2:3, QM:128] = positive[:, 2 * QM : 3 * QM]
    tts[3:4, :] = jnp.zeros((1, 128), F32)
    totals = [near_slab(tts, ttr.at[4 - k], k) for k in (1, -1, 2, -2, 3, -3, 4, -4)]

    terms = lax.dot_general(
        eb[...], pb[...], (((0,), (0,)), ((), ())), preferred_element_type=F32
    )
    returns = []
    for k in (2, -2, 1, -1):
        gs[2 + k] = terms[(2 + k) * QM : (3 + k) * QM].astype(BF)
        returns.append(near_slab(gs.at[2 + k], gr.at[2 - k], k))
    own_terms = terms[2 * QM : 3 * QM]

    ttr[4] = tts[...]
    heads[0].wait_recv()
    theirs = head.at[rows(256, opp)]
    heads.append(Send(theirs, theirs, to_sib))
    for copy in totals:
        copy.wait_recv()
    for k in range(-2, 3):
        rest = jnp.zeros((1, QM), F32)
        for j in range(-2, 3):
            n = 2 - j
            rest = rest + ttr[k + j + 4][n // 2 : n // 2 + 1, (n % 2) * QM : (n % 2 + 1) * QM]
        whole = rest + ttr[k + 4][2:3, QM:128]
        lanes = slice((2 + k) * QM, (3 + k) * QM)
        scale = auxc[4:5, lanes] / (whole * TAU)
        auxc[6:7, lanes] = jnp.where(inside(k), scale, 0.0)
        if k == 0:
            own_rest, own_whole = rest, whole
            auxc[7:8, lanes] = scale * rest
        else:
            auxc[7:8, lanes] = jnp.zeros((1, QM), F32)

    for tile in range(4):
        here = slice(tile * PM, (tile + 1) * PM)
        is_positive = (slot_ids + tile * PM).astype(F32) == auxc[5:6, :]
        coefficient = jnp.where(is_positive, -auxc[7:8, :], ef[here] * auxc[6:7, :])
        part = jnp.dot(coefficient.astype(BF), qb[...], preferred_element_type=F32)
        ppf[here] = part
        pps[here] = part.astype(BF)
    p1 = Send(pps.at[rows(PM, osib)], pr.at[1], to_sib)
    p0 = Send(pps.at[rows(PM, sib)], pr.at[0], to_sib)
    p1.wait_recv()
    py[...] = (ppf[rows(PM, opp)] + pr[1].astype(F32)).astype(BF)
    p2 = Send(py, pz, to_opp)

    def tangent(unit, norm, grad):
        radial = jnp.sum(unit * grad, axis=1, keepdims=True)
        return ((grad - unit * radial) / norm).astype(BF)

    eye = lax.broadcasted_iota(jnp.int32, (QM, QM), 0) == lax.broadcasted_iota(
        jnp.int32, (QM, QM), 1
    )

    def column(row):
        return jnp.sum(jnp.where(eye, row, 0.0), axis=1, keepdims=True)

    one_hot = (
        lax.broadcasted_iota(jnp.int32, (4 * PM, QM), 0).astype(F32) == wanted
    ).astype(F32).astype(BF)
    chosen = lax.dot_general(
        one_hot, pb[...], (((0,), (0,)), ((), ())), preferred_element_type=F32
    )
    scale = column(weight / (own_whole * TAU))
    drop = column(weight * own_rest / (own_whole * TAU))
    for copy in returns:
        copy.wait_recv()
    for k in (0, 1, 3, 4):
        own_terms = own_terms + gr[k].astype(F32)
    pgo[0:QM] = tangent(unit_q[...], norm_q[...], own_terms * scale - chosen * drop)
    p0.wait_recv()
    p2.wait_recv()
    summed = ppf[rows(PM, m)] + pr[0].astype(F32) + pz[...].astype(F32)
    pgo[QM:] = tangent(unit_p[...], norm_p[...], summed)

    for copy in wide:
        copy.wait_recv()

    def cols(size, index):
        return pl.ds(pl.multiple_of(index * size, size), size)

    def term(block, half, owner):
        features = cols(128, (2 * block + owner) * 2 + half)
        return lax.dot_general(
            xo[:, features], pgo[...], (((0,), (0,)), ((), ())), preferred_element_type=F32
        )

    pairs = []
    for half in range(2):
        for block in range(2):
            there = slice(half * 128, (half + 1) * 128)
            tsend[block, there] = term(block, half, 1 - core).astype(BF)
            pairs.append(Send(tsend.at[block, there], trecv.at[block, there], to_sib))
    for half in range(2):
        for block in range(2):
            there = slice(half * 128, (half + 1) * 128)
            hf[block, there] = term(block, half, core)

    first = []
    for half in range(2):
        there = slice(half * 128, (half + 1) * 128)
        for block in range(2):
            pairs[2 * half + block].wait_recv()
            total = hf[block, there] + trecv[block, there].astype(F32)
            hf[block, there] = total
            hb[block, there] = total.astype(BF)
        if half == 0:
            for k in (2, 1, 3):
                first.append(
                    Send(hb.at[:, there, cols(256, (xi + k) % 4)], ax.at[k - 1], at_x(k))
                )
        else:
            first.append(Send(hb.at[low, there, cols(512, 1 - high)], cy.at[2], to_high))
            first.append(Send(hb.at[1 - low, there, cols(512, high)], cy.at[0], to_opp))
            first.append(Send(hb.at[1 - low, there, cols(512, 1 - high)], cy.at[1], to_back))

    for copy in heads[1:]:
        copy.wait_recv()
    eo[...] = lax.dot_general(
        pgo[...], head[...], (((1,), (1,)), ((), ())), preferred_element_type=F32
    ).astype(BF)
    oq_ref[rows(QM, m)] = eo[0:QM, cols(256, m)]
    op_ref[rows(PM, m)] = eo[QM:, cols(256, m)]

    def spread(member, device):
        return [
            Send(eo.at[0:QM, cols(256, member)], oq_ref.at[rows(QM, m)], device),
            Send(eo.at[QM : QM + PM, cols(256, member)], op_ref.at[rows(PM, m)], device),
        ]

    outs = spread(sib, to_sib)

    for copy in first[:3]:
        copy.wait_recv()
    total = hf[:, 0:128, cols(256, xi)]
    for k in range(3):
        total = total + ax[k].astype(F32)
    a1f[...] = total
    a1[...] = total.astype(BF)
    second = [
        Send(a1.at[low, :, cols(128, 1 - high)], ay.at[2], to_high),
        Send(a1.at[1 - low, :, cols(128, high)], ay.at[0], to_opp),
        Send(a1.at[1 - low, :, cols(128, 1 - high)], ay.at[1], to_back),
    ]
    for copy in first[3:]:
        copy.wait_recv()
    total = hf[low, 128:256, cols(512, high)]
    for k in range(3):
        total = total + cy[k].astype(F32)
    c1f[...] = total
    c1[...] = total.astype(BF)
    for k in (2, 1, 3):
        second.append(Send(c1.at[:, cols(128, (xi + k) % 4)], cx.at[k - 1], at_x(k)))
    for copy in second:
        copy.wait_recv()
    total = a1f[low, :, cols(128, high)]
    for k in range(3):
        total = total + ay[k].astype(F32)
    e1f[0:128] = total
    e1[0:128] = total.astype(BF)
    total = c1f[:, cols(128, xi)]
    for k in range(3):
        total = total + cx[k].astype(F32)
    e1f[128:256] = total
    e1[128:256] = total.astype(BF)
    third = []
    for k in (4, 3, 5, 2, 6, 1, 7):
        third.append(Send(e1.at[rows(32, (zi + k) % 8)], ez.at[k - 1], at_z(k)))
    outs += spread(opp, to_opp) + spread(osib, to_osib)
    for copy in third:
        copy.wait_recv()
    total = e1f[rows(32, zi)]
    for k in range(7):
        total = total + ez[k].astype(F32)
    gz[rows(32, zi)] = total.astype(BF)
    fourth = []
    for k in (4, 3, 5, 2, 6, 1, 7):
        fourth.append(Send(gz.at[rows(32, zi)], gz.at[rows(32, zi)], at_z(k)))
    for copy in fourth:
        copy.wait_recv()
    upper = cols(128, 2 * xi + high)
    lower = cols(128, 4 * high + xi)
    oh_ref[0:128, upper] = gz[0:128]
    oh_ref[128:256, lower] = gz[128:256]
    mine = oh_ref.at[0:128, upper]
    fifth = [Send(mine, mine, to_high)]
    mine = oh_ref.at[128:256, lower]
    for k in (2, 1, 3):
        fifth.append(Send(mine, mine, at_x(k)))
    fifth[0].wait_recv()
    last = []
    mine = oh_ref.at[0:128, cols(256, xi)]
    for k in (2, 1, 3):
        last.append(Send(mine, mine, at_x(k)))
    for copy in fifth[1:]:
        copy.wait_recv()
    mine = oh_ref.at[128:256, cols(512, high)]
    last.append(Send(mine, mine, to_high))
    for copy in outs + last:
        copy.wait_recv()
    for copy in sent:
        copy.wait_send()


def body(query_emb, passage_emb, head, fn_mask, counts, positive_slot, query_weight):
    vmem = pl.BlockSpec(memory_space=pltpu.VMEM)
    hbm = pl.BlockSpec(memory_space=pl.ANY)
    smem = pl.BlockSpec(memory_space=pltpu.SMEM)

    def half(*shape):
        return pltpu.VMEM(shape, BF)

    def full(*shape):
        return pltpu.VMEM(shape, F32)

    query_grad, passage_grad, head_grad = pl.pallas_call(
        kernel,
        out_shape=(
            jax.ShapeDtypeStruct((256, 256), BF),
            jax.ShapeDtypeStruct((512, 256), BF),
            jax.ShapeDtypeStruct((256, D), BF),
        ),
        in_specs=[hbm, hbm, hbm, hbm, smem, hbm, hbm],
        out_specs=(vmem, vmem, vmem),
        scratch_shapes=[
            half(256, 256), half(512, 256), half(D, D),
            pltpu.VMEM((5, 4, 256), jnp.int32), pltpu.VMEM((1, 256), jnp.int32), full(1, 256),
            half(256, D), half(512, D), half(2, QM, D), half(2, PM, D),
            half(QM, D), half(PM, D), half(QM, D), half(PM, D),
            full(QM, D), full(PM, D), full(QM, 1), full(PM, 1),
            half(NQ, D), half(4 * PM, D), full(5, 8, 128), full(5, 8, 128), full(8, NQ),
            full(4 * PM, NQ), half(4 * PM, NQ), full(4, 128), full(9, 4, 128),
            half(5, QM, D), half(5, QM, D),
            half(512, D), full(512, D), half(2, PM, D), half(PM, D), half(PM, D),
            half(QM + PM, D), half(QM + PM, D), half(QM + PM, D),
            half(2, 256, D), half(2, 256, D), full(2, 256, D), half(2, 256, D),
            half(3, 2, 128, 256), half(3, 128, 512),
            full(2, 128, 256), full(128, 512), half(2, 128, 256), half(128, 512),
            half(3, 128, 128), half(3, 128, 128), full(256, 128), half(256, 128),
            half(7, 32, 128), half(256, 128),
            pltpu.SemaphoreType.DMA((6,)),
            pltpu.SemaphoreType.DMA((SEMS,)), pltpu.SemaphoreType.DMA((SEMS,)),
        ],
        compiler_params=pltpu.CompilerParams(
            collective_id=0, has_side_effects=True, vmem_limit_bytes=48 << 20
        ),
        cost_estimate=pl.CostEstimate(flops=3 << 30, bytes_accessed=4 << 20, transcendentals=0),
    )(
        query_emb, passage_emb, head, jnp.transpose(fn_mask, (1, 2, 0)), counts,
        positive_slot.reshape(1, -1), query_weight.reshape(1, -1),
    )
    return query_grad, passage_grad, head_grad.astype(F32)


def solution(mesh):
    return jax.shard_map(
        body,
        mesh=mesh,
        in_specs=(
            P("slab", "mp"), P("slab", "mp"), P("mp", None), P("slab", None, None),
            P(), P("slab"), P("slab"),
        ),
        out_specs=(P("slab", "mp"), P("slab", "mp"), P("mp", None)),
        check_vma=False,
    )
```

time: 104 us -> 90.4 us (0.87)
  Pallas kernels: 96.3 us -> 82.7 us
  other arithmetic: 0 us -> 1.09 us
    pallas_call x1, Pallas kernels: 96.3 us -> 82.7 us  [body(): pl.pallas_call(kernel, out_shape=(jax.ShapeDtypeStruct((256, 256), BF), j...]
    convert_element_type x0 -> x1, other arithmetic: none -> 1.09 us  [body(): return (query_grad, passage_grad, head_grad.astype(F32))]
    unnamed x17 -> x16, local copies, waits for them, and re-layouts: 6.62 us -> 5.65 us
where the time goes in v2:
time: 90.4 us; the launch traced here: 90.1 us
  Pallas kernels  82.7 us (91%)
  local copies, waits for them, and re-layouts  5.65 us (6%)
  other arithmetic  1.09 us (1%)
    pallas_call x1, Pallas kernels, body(): pl.pallas_call(kernel, out_shape=(jax.ShapeDtypeStruct((256, 256), BF), j...  82.7 us
    unnamed x16, local copies, waits for them, and re-layouts  5.65 us

profile of v2, /device:TPU:8, one launch (start us, length us, event | category | flops | bytes accessed | tf_op | source)
XLA Modules:
  0.0 90.1 jit_solution(709962282100062733)
XLA Ops:
  0.6 0.0 copy-start.5
  0.6 0.0 copy-start.4
  0.7 0.0 copy-start.6
  0.7 0.7 copy-done.5
  1.3 0.0 copy-done.4
  1.3 0.0 copy-done.6
  1.3 0.0 copy-start
  1.3 1.0 %copy-done = bf16[256,1024]{1,0:T(8,128)(2,1)S(1)} copy-done((bf16[256,1024]{1,0:T(8,128)(2,1)S(1)}, bf16[256,1024]{1,0:T(8,128)(2,1)}, u32[]{:S(2)}) %copy-start) | copy-done | bytes 524312
  2.4 0.0 copy-start.1
  2.4 0.9 %copy-done.1 = bf16[512,256]{1,0:T(8,128)(2,1)S(1)} copy-done((bf16[512,256]{1,0:T(8,128)(2,1)S(1)}, bf16[512,256]{1,0:T(8,128)(2,1)}, u32[]{:S(2)}) %copy-start.1) | copy-done | bytes 262168
  3.3 0.0 copy-start.2
  3.3 0.9 %copy-done.2 = bf16[256,256]{1,0:T(8,128)(2,1)S(1)} copy-done((bf16[256,256]{1,0:T(8,128)(2,1)S(1)}, bf16[256,256]{1,0:T(8,128)(2,1)}, u32[]{:S(2)}) %copy-start.2) | copy-done | bytes 131096
  4.2 0.0 copy-start.3
  4.2 0.7 copy-done.3
  5.0 82.7 %shard_map.94 = (bf16[256,256]{1,0:T(8,128)(2,1)S(1)}, bf16[512,256]{1,0:T(8,128)(2,1)S(1)}, bf16[256,1024]{1,0:T(8,128)(2,1)S(1)}) custom-call(bf16[256,256]{1,0:T(8,128)(2,1)S(1)} %copy-done.2, bf16[512,256]{1,0:T(8,128)(2,1)S(1)} %copy-done.1, bf16[256,1024]{1,0:T(8,128)(2,1)S(1)} %copy-done, s32[5,4,256]{2,1,0:T(4,128)S(1)} %bitcast.3, s32[64]{0:T(128)S(1)} %copy-done.6, ...), custom_call_target="tpu_custom_call" | custom-call | flops 3221225472 | bytes 4194304 | tf_op jit(solution)/shard_map/pallas_call | solution.py:443
  87.7 1.1 %convert_element_type.3 = f32[256,1024]{1,0:T(8,128)} convert(bf16[256,1024]{1,0:T(8,128)(2,1)S(1)} %get-tuple-element.8) | non-fusion elementwise | flops 262144 | bytes 1572864 | tf_op jit(solution)/shard_map/convert_element_type | solution.py:479
  88.8 0.7 copy.12
  89.4 0.7 copy.13
Async XLA Ops:
  0.6 0.7 copy-start.5
  0.6 0.7 copy-start.4
  0.7 0.7 copy-start.6
  1.3 1.0 %copy-start = (bf16[256,1024]{1,0:T(8,128)(2,1)S(1)}, bf16[256,1024]{1,0:T(8,128)(2,1)}, u32[]{:S(2)}) copy-start(bf16[256,1024]{1,0:T(8,128)(2,1)} %head_hbm.1) | copy-start | bytes 1572868
  2.4 0.9 %copy-start.1 = (bf16[512,256]{1,0:T(8,128)(2,1)S(1)}, bf16[512,256]{1,0:T(8,128)(2,1)}, u32[]{:S(2)}) copy-start(bf16[512,256]{1,0:T(8,128)(2,1)} %p_hbm.1) | copy-start | bytes 786436
  3.3 0.9 %copy-start.2 = (bf16[256,256]{1,0:T(8,128)(2,1)S(1)}, bf16[256,256]{1,0:T(8,128)(2,1)}, u32[]{:S(2)}) copy-start(bf16[256,256]{1,0:T(8,128)(2,1)} %q_hbm.1) | copy-start | bytes 393220
  4.2 0.7 copy-start.3

commit v3 on v2

--- a/solution.py
+++ b/solution.py
@@ -18,14 +18,13 @@
 
 
 def kernel(
-    q_hbm, p_hbm, head_hbm, mask_hbm, counts_ref, pos_hbm, weight_hbm,
+    q_hbm, p_hbm, head_hbm, mask_hbm, counts_hbm, pos_hbm, weight_hbm,
     oq_ref, op_ref, oh_ref,
-    q_ref, p_ref, head, mask_ref, pos_ref, weight_ref,
-    part_q, part_p, rq, rp, yq, yp, zq, zp,
-    unit_q, unit_p, norm_q, norm_p,
+    q_ref, p_ref, head, mask_ref, counts_ref, pos_ref, weight_ref,
+    part_q, rq, yq, zq, xh, unit_q, unit_p, norm_q, norm_p,
     qb, pb, auxs, auxr, auxc, ef, eb, tts, ttr, gs, gr,
-    pps, ppf, pr, py, pz, xo, pgo, eo,
-    tsend, trecv, hf, hb, ax, cy, a1f, c1f, a1, c1, ay, cx, e1f, e1, ez, gz,
+    pps, pr, py, pz, xo, pgt, eo,
+    hf, hb, ax, cy, a1f, c1f, a1, c1, ay, cx, e1f, e1, ez, gz,
     lsem, ssem, rsem,
 ):
     slab = lax.axis_index("slab")
@@ -35,6 +34,8 @@
     opp = 2 * (1 - low) + core
     osib = 2 * (1 - low) + 1 - core
     high, xi, zi = slab // 32, (slab // 8) % 4, slab % 8
+    p_own, p_sib = 2 * core + low, 2 * (1 - core) + low
+    p_opp, p_osib = 2 * core + 1 - low, 2 * (1 - core) + 1 - low
 
     def at_slab(distance):
         there = (slab + distance + 64) % 64
@@ -92,7 +93,8 @@
         pltpu.make_async_copy(src, dst, lsem.at[i])
         for i, (src, dst) in enumerate((
             (q_hbm, q_ref), (head_hbm, head.at[rows(256, m)]), (p_hbm, p_ref),
-            (mask_hbm, mask_ref), (pos_hbm, pos_ref), (weight_hbm, weight_ref),
+            (mask_hbm, mask_ref), (counts_hbm, counts_ref), (pos_hbm, pos_ref),
+            (weight_hbm, weight_ref),
         ))
     ]
     for copy in loads:
@@ -114,18 +116,29 @@
     pl.semaphore_wait(barrier, len(peers))
     q1 = Send(part_q.at[rows(QM, osib)], rq.at[1], to_sib)
     q0 = Send(part_q.at[rows(QM, sib)], rq.at[0], to_sib)
-    mine = head.at[rows(256, m)]
-    heads = [Send(mine, mine, to_back)]
-    loads[2].wait()
-    part_p[...] = jnp.dot(p_ref[...], own_head, preferred_element_type=F32).astype(BF)
-    p1 = Send(part_p.at[rows(PM, osib)], rp.at[1], to_sib)
-    p0 = Send(part_p.at[rows(PM, sib)], rp.at[0], to_sib)
+
+    def head_rows(member, start, size):
+        return head.at[pl.ds(pl.multiple_of(member * 256 + start, 16), size)]
+
+    heads = []
+    for start, size in ((0, 112), (112, 112)):
+        mine = head_rows(m, start, size)
+        heads.append(Send(mine, mine, to_back))
+    near_head = Send(head_rows(m, 0, 256), head_rows(m, 0, 256), to_sib)
     q1.wait_recv()
     yq[...] = (part_q[rows(QM, opp)].astype(F32) + rq[1].astype(F32)).astype(BF)
     q2 = Send(yq, zq, to_opp)
-    p1.wait_recv()
-    yp[...] = (part_p[rows(PM, opp)].astype(F32) + rp[1].astype(F32)).astype(BF)
-    p2 = Send(yp, zp, to_opp)
+
+    loads[2].wait()
+    feature = rows(256, m)
+    wide = [
+        Send(p_ref.at[rows(256, core)], xh.at[:, feature], to_opp),
+        Send(p_ref.at[rows(256, 1 - core)], xh.at[:, feature], to_osib),
+        Send(p_ref.at[rows(256, 1 - core)], xh.at[:, feature], to_sib),
+    ]
+    xh[:, feature] = p_ref[rows(256, core)]
+    mine = head_rows(m, 224, 32)
+    heads.append(Send(mine, mine, to_opp))
 
     def own_lanes(value):
         quarters = [value[:, k * QM : (k + 1) * QM] for k in range(4)]
@@ -145,8 +158,10 @@
     for k in range(5):
         auxs[k, 0:4, 0:QM] = own_lanes(mask_ref[k].astype(F32))
         auxs[k, 4:5, 0:QM] = weight
-    xo[0:QM, rows(256, m)] = q_ref[rows(QM, m)]
-    xo[QM:, rows(256, m)] = p_ref[rows(PM, m)]
+    xo[0:QM, rows(256, low)] = q_ref[rows(QM, m)]
+    xo[QM:192, rows(256, low)] = p_ref[rows(PM, p_own)]
+    xo[192 : 192 + QM, rows(256, low)] = q_ref[rows(QM, sib)]
+    xo[192 + QM :, rows(256, low)] = p_ref[rows(PM, p_sib)]
 
     def normalise(projected):
         norm = jnp.sqrt(jnp.sum(projected * projected, axis=1, keepdims=True) + EPS)
@@ -167,35 +182,36 @@
         )
         auxes.append(near_slab(auxs.at[2 + k], auxr.at[2 - k], k))
 
-    p0.wait_recv()
-    p2.wait_recv()
-    unit, norm = normalise(
-        part_p[rows(PM, m)].astype(F32) + rp[0].astype(F32) + zp[...].astype(F32)
-    )
+    wide_q = [
+        Send(q_ref.at[rows(QM, member)], xo.at[first : first + QM, rows(256, low)], to_opp)
+        for first, member in ((0, opp), (192, osib))
+    ]
+
+    def chip_part(chip):
+        features = rows(512, chip)
+        return jnp.dot(xh[:, features], head[features], preferred_element_type=F32)
+
+    wide[2].wait_recv()
+    near_head.wait_recv()
+    projected = chip_part(low)
+    far_heads = []
+    for copy, (start, size) in ((heads[0], (0, 112)), (heads[2], (224, 32)), (heads[1], (112, 112))):
+        copy.wait_recv()
+        theirs = head_rows(opp, start, size)
+        far_heads.append(Send(theirs, theirs, to_sib))
+    for copy in wide[:2] + far_heads:
+        copy.wait_recv()
+    unit, norm = normalise(projected + chip_part(1 - low))
     unit_p[...] = unit
     norm_p[...] = norm
-    pb[rows(PM, m)] = unit.astype(BF)
-
-    def piece(member, part):
-        return pb.at[pl.ds(pl.multiple_of(member * PM + part * 64, 64), 64)]
-
-    over = [Send(piece(m, h), piece(m, h), to_opp) for h in range(2)]
-    near = Send(pb.at[rows(PM, m)], pb.at[rows(PM, m)], to_sib)
-    wide = []
-    for member, device in ((opp, to_opp), (osib, to_osib), (sib, to_sib)):
-        wide.append(
-            Send(q_ref.at[rows(QM, member)], xo.at[0:QM, rows(256, m)], device)
-        )
-        wide.append(
-            Send(p_ref.at[rows(PM, member)], xo.at[QM : QM + PM, rows(256, m)], device)
-        )
-    far = []
-    for h in range(2):
-        over[h].wait_recv()
-        far.append(Send(piece(opp, h), piece(opp, h), to_sib))
-    heads.append(Send(mine, mine, to_sib))
-    for copy in [near] + far:
-        copy.wait_recv()
+    pb[rows(256, core)] = unit.astype(BF)
+    mine = pb.at[rows(256, core)]
+    near = Send(mine, mine, to_sib)
+    xo[QM:192, rows(256, 1 - low)] = xh[rows(PM, low), rows(256, opp)]
+    wide_q.append(
+        Send(xh.at[rows(PM, low), rows(256, osib)], xo.at[192 + QM : 384, rows(256, 1 - low)], to_sib)
+    )
+    near.wait_recv()
     for copy in queries + auxes:
         copy.wait_recv()
 
@@ -238,9 +254,6 @@
     own_terms = terms[2 * QM : 3 * QM]
 
     ttr[4] = tts[...]
-    heads[0].wait_recv()
-    theirs = head.at[rows(256, opp)]
-    heads.append(Send(theirs, theirs, to_sib))
     for copy in totals:
         copy.wait_recv()
     for k in range(-2, 3):
@@ -258,18 +271,23 @@
         else:
             auxc[7:8, lanes] = jnp.zeros((1, QM), F32)
 
-    for tile in range(4):
-        here = slice(tile * PM, (tile + 1) * PM)
-        is_positive = (slot_ids + tile * PM).astype(F32) == auxc[5:6, :]
-        coefficient = jnp.where(is_positive, -auxc[7:8, :], ef[here] * auxc[6:7, :])
-        part = jnp.dot(coefficient.astype(BF), qb[...], preferred_element_type=F32)
-        ppf[here] = part
-        pps[here] = part.astype(BF)
-    p1 = Send(pps.at[rows(PM, osib)], pr.at[1], to_sib)
-    p0 = Send(pps.at[rows(PM, sib)], pr.at[0], to_sib)
-    p1.wait_recv()
-    py[...] = (ppf[rows(PM, opp)] + pr[1].astype(F32)).astype(BF)
-    p2 = Send(py, pz, to_opp)
+    def passage_terms(index):
+        is_positive = (slot_ids + index * PM).astype(F32) == auxc[5:6, :]
+        coefficient = jnp.where(is_positive, -auxc[7:8, :], ef[rows(PM, index)] * auxc[6:7, :])
+        return jnp.dot(coefficient.astype(BF), qb[...], preferred_element_type=F32)
+
+    pps[1] = passage_terms(p_osib).astype(BF)
+    pieces = [slice(0, 64), slice(64, 128)]
+    p1 = [Send(pps.at[1, piece], pr.at[1, piece], to_sib) for piece in pieces]
+    part = passage_terms(p_opp)
+    p2 = []
+    for copy, piece in zip(p1, pieces):
+        copy.wait_recv()
+        py[piece] = (part[piece] + pr[1, piece].astype(F32)).astype(BF)
+        p2.append(Send(py.at[piece], pz.at[piece], to_opp))
+    pps[0] = passage_terms(p_sib).astype(BF)
+    p0 = Send(pps.at[0], pr.at[0], to_sib)
+    own_part = passage_terms(p_own)
 
     def tangent(unit, norm, grad):
         radial = jnp.sum(unit * grad, axis=1, keepdims=True)
@@ -294,41 +312,28 @@
         copy.wait_recv()
     for k in (0, 1, 3, 4):
         own_terms = own_terms + gr[k].astype(F32)
-    pgo[0:QM] = tangent(unit_q[...], norm_q[...], own_terms * scale - chosen * drop)
-    p0.wait_recv()
-    p2.wait_recv()
-    summed = ppf[rows(PM, m)] + pr[0].astype(F32) + pz[...].astype(F32)
-    pgo[QM:] = tangent(unit_p[...], norm_p[...], summed)
-
-    for copy in wide:
-        copy.wait_recv()
+    pgt[0:QM] = tangent(unit_q[...], norm_q[...], own_terms * scale - chosen * drop)
+    shared = [Send(pgt.at[0:QM], pgt.at[192 : 192 + QM], to_sib)]
+    for copy in [p0] + p2:
+        copy.wait_recv()
+    summed = own_part + pr[0].astype(F32) + pz[...].astype(F32)
+    pgt[QM:192] = tangent(unit_p[rows(PM, low)], norm_p[rows(PM, low)], summed)
+    shared.append(Send(pgt.at[QM:192], pgt.at[192 + QM : 384], to_sib))
 
     def cols(size, index):
         return pl.ds(pl.multiple_of(index * size, size), size)
 
-    def term(block, half, owner):
-        features = cols(128, (2 * block + owner) * 2 + half)
-        return lax.dot_general(
-            xo[:, features], pgo[...], (((0,), (0,)), ((), ())), preferred_element_type=F32
-        )
-
-    pairs = []
-    for half in range(2):
-        for block in range(2):
-            there = slice(half * 128, (half + 1) * 128)
-            tsend[block, there] = term(block, half, 1 - core).astype(BF)
-            pairs.append(Send(tsend.at[block, there], trecv.at[block, there], to_sib))
-    for half in range(2):
-        for block in range(2):
-            there = slice(half * 128, (half + 1) * 128)
-            hf[block, there] = term(block, half, core)
+    for copy in wide_q + shared:
+        copy.wait_recv()
 
     first = []
     for half in range(2):
         there = slice(half * 128, (half + 1) * 128)
         for block in range(2):
-            pairs[2 * half + block].wait_recv()
-            total = hf[block, there] + trecv[block, there].astype(F32)
+            features = slice(block * 256 + half * 128, block * 256 + (half + 1) * 128)
+            total = lax.dot_general(
+                xo[:, features], pgt[...], (((0,), (0,)), ((), ())), preferred_element_type=F32
+            )
             hf[block, there] = total
             hb[block, there] = total.astype(BF)
         if half == 0:
@@ -341,18 +346,16 @@
             first.append(Send(hb.at[1 - low, there, cols(512, high)], cy.at[0], to_opp))
             first.append(Send(hb.at[1 - low, there, cols(512, 1 - high)], cy.at[1], to_back))
 
-    for copy in heads[1:]:
-        copy.wait_recv()
     eo[...] = lax.dot_general(
-        pgo[...], head[...], (((1,), (1,)), ((), ())), preferred_element_type=F32
+        pgt[0:192], head[...], (((1,), (1,)), ((), ())), preferred_element_type=F32
     ).astype(BF)
     oq_ref[rows(QM, m)] = eo[0:QM, cols(256, m)]
-    op_ref[rows(PM, m)] = eo[QM:, cols(256, m)]
+    op_ref[rows(PM, p_own)] = eo[QM:, cols(256, m)]
 
     def spread(member, device):
         return [
             Send(eo.at[0:QM, cols(256, member)], oq_ref.at[rows(QM, m)], device),
-            Send(eo.at[QM : QM + PM, cols(256, member)], op_ref.at[rows(PM, m)], device),
+            Send(eo.at[QM : QM + PM, cols(256, member)], op_ref.at[rows(PM, p_own)], device),
         ]
 
     outs = spread(sib, to_sib)
@@ -431,8 +434,7 @@
 
 def body(query_emb, passage_emb, head, fn_mask, counts, positive_slot, query_weight):
     vmem = pl.BlockSpec(memory_space=pltpu.VMEM)
-    hbm = pl.BlockSpec(memory_space=pl.ANY)
-    smem = pl.BlockSpec(memory_space=pltpu.SMEM)
+    hbm = pl.BlockSpec(memory_space=pltpu.HBM)
 
     def half(*shape):
         return pltpu.VMEM(shape, BF)
@@ -447,35 +449,38 @@
             jax.ShapeDtypeStruct((512, 256), BF),
             jax.ShapeDtypeStruct((256, D), BF),
         ),
-        in_specs=[hbm, hbm, hbm, hbm, smem, hbm, hbm],
+        in_specs=[hbm] * 7,
         out_specs=(vmem, vmem, vmem),
         scratch_shapes=[
             half(256, 256), half(512, 256), half(D, D),
-            pltpu.VMEM((5, 4, 256), jnp.int32), pltpu.VMEM((1, 256), jnp.int32), full(1, 256),
-            half(256, D), half(512, D), half(2, QM, D), half(2, PM, D),
-            half(QM, D), half(PM, D), half(QM, D), half(PM, D),
-            full(QM, D), full(PM, D), full(QM, 1), full(PM, 1),
+            pltpu.VMEM((5, 4, 256), jnp.int32), pltpu.SMEM((64,), jnp.int32),
+            pltpu.VMEM((1, 256), jnp.int32), full(1, 256),
+            half(256, D), half(2, QM, D), half(QM, D), half(QM, D), half(256, D),
+            full(QM, D), full(256, D), full(QM, 1), full(256, 1),
             half(NQ, D), half(4 * PM, D), full(5, 8, 128), full(5, 8, 128), full(8, NQ),
             full(4 * PM, NQ), half(4 * PM, NQ), full(4, 128), full(9, 4, 128),
             half(5, QM, D), half(5, QM, D),
-            half(512, D), full(512, D), half(2, PM, D), half(PM, D), half(PM, D),
-            half(QM + PM, D), half(QM + PM, D), half(QM + PM, D),
-            half(2, 256, D), half(2, 256, D), full(2, 256, D), half(2, 256, D),
+            half(2, PM, D), half(2, PM, D), half(PM, D), half(PM, D),
+            half(384, 512), half(384, D), half(192, D),
+            full(2, 256, D), half(2, 256, D),
             half(3, 2, 128, 256), half(3, 128, 512),
             full(2, 128, 256), full(128, 512), half(2, 128, 256), half(128, 512),
             half(3, 128, 128), half(3, 128, 128), full(256, 128), half(256, 128),
             half(7, 32, 128), half(256, 128),
-            pltpu.SemaphoreType.DMA((6,)),
+            pltpu.SemaphoreType.DMA((7,)),
             pltpu.SemaphoreType.DMA((SEMS,)), pltpu.SemaphoreType.DMA((SEMS,)),
         ],
         compiler_params=pltpu.CompilerParams(
             collective_id=0, has_side_effects=True, vmem_limit_bytes=48 << 20
         ),
         cost_estimate=pl.CostEstimate(flops=3 << 30, bytes_accessed=4 << 20, transcendentals=0),
-    )(
-        query_emb, passage_emb, head, jnp.transpose(fn_mask, (1, 2, 0)), counts,
-        positive_slot.reshape(1, -1), query_weight.reshape(1, -1),
-    )
+    )(*[
+        pltpu.with_memory_space_constraint(value, pltpu.HBM)
+        for value in (
+            query_emb, passage_emb, head, jnp.transpose(fn_mask, (1, 2, 0)), counts,
+            positive_slot.reshape(1, -1), query_weight.reshape(1, -1),
+        )
+    ])
     return query_grad, passage_grad, head_grad.astype(F32)
 
 

time: 90.4 us -> 85.9 us (0.950)
  local copies, waits for them, and re-layouts: 5.65 us -> 1.36 us
    unnamed x16 -> x2, local copies, waits for them, and re-layouts: 5.65 us -> 1.36 us
where the time goes in v3:
time: 85.9 us; the launch traced here: 85.4 us
  Pallas kernels  82.3 us (96%)
  local copies, waits for them, and re-layouts  1.36 us (2%)
  other arithmetic  1.09 us (1%)
    pallas_call x1, Pallas kernels, body(): pl.pallas_call(kernel, out_shape=(jax.ShapeDtypeStruct((256, 256), BF), j...  82.3 us

profile of v3, /device:TPU:8, one launch (start us, length us, event | category | flops | bytes accessed | tf_op | source)
XLA Modules:
  0.0 85.4 jit_solution(8848687076060325175)
XLA Ops:
  0.6 82.3 %shard_map.94 = (bf16[256,256]{1,0:T(8,128)(2,1)S(1)}, bf16[512,256]{1,0:T(8,128)(2,1)S(1)}, bf16[256,1024]{1,0:T(8,128)(2,1)S(1)}) custom-call(bf16[256,256]{1,0:T(8,128)(2,1)} %q_hbm.1, bf16[512,256]{1,0:T(8,128)(2,1)} %p_hbm.1, bf16[256,1024]{1,0:T(8,128)(2,1)} %head_hbm.1, s32[5,4,256]{2,1,0:T(4,128)} %bitcast.3, s32[64]{0:T(128)} %counts_hbm.1, ...), custom_call_target="tpu_custom_call" | custom-call | flops 3221225472 | bytes 4194304 | tf_op jit(solution)/shard_map/pallas_call | solution.py:445
  82.9 1.1 %convert_element_type.3 = f32[256,1024]{1,0:T(8,128)} convert(bf16[256,1024]{1,0:T(8,128)(2,1)S(1)} %get-tuple-element.8) | non-fusion elementwise | flops 262144 | bytes 1572864 | tf_op jit(solution)/shard_map/convert_element_type | solution.py:484
  84.0 0.7 copy.12
  84.7 0.7 copy.13

commit v4 on v3

--- a/solution.py
+++ b/solution.py
@@ -11,7 +11,7 @@
 QM = 64
 PM = 128
 NQ = 5 * QM
-SEMS = 112
+SEMS = 128
 MESH = pl.DeviceIdType.MESH
 BF = jnp.bfloat16
 F32 = jnp.float32
@@ -24,7 +24,7 @@
     part_q, rq, yq, zq, xh, unit_q, unit_p, norm_q, norm_p,
     qb, pb, auxs, auxr, auxc, ef, eb, tts, ttr, gs, gr,
     pps, pr, py, pz, xo, pgt, eo,
-    hf, hb, ax, cy, a1f, c1f, a1, c1, ay, cx, e1f, e1, ez, gz,
+    hf, hb, ax, cy, a1f, c1f, a1, c1, ay, cx, e1f, e1, ez, gz, ga,
     lsem, ssem, rsem,
 ):
     slab = lax.axis_index("slab")
@@ -44,6 +44,9 @@
     def at_x(step):
         return (high * 32 + ((xi + step) % 4) * 8 + zi, m)
 
+    def at_high_x(step):
+        return ((1 - high) * 32 + ((xi + step) % 4) * 8 + zi, m)
+
     def at_z(step):
         return (high * 32 + xi * 8 + (zi + step) % 8, m)
 
@@ -55,6 +58,7 @@
     peers = [to_sib, to_opp, to_osib, to_high, to_back]
     peers += [at_slab(k) for k in (-4, -3, -2, -1, 1, 2, 3, 4)]
     peers += [at_x(k) for k in range(1, 4)] + [at_z(k) for k in range(1, 8)]
+    peers += [at_high_x(k) for k in range(1, 4)]
     sent = []
 
     class Send:
@@ -118,11 +122,12 @@
     q0 = Send(part_q.at[rows(QM, sib)], rq.at[0], to_sib)
 
     def head_rows(member, start, size):
-        return head.at[pl.ds(pl.multiple_of(member * 256 + start, 16), size)]
-
+        return head.at[pl.ds(pl.multiple_of(member * 256 + start, 32), size)]
+
+    half_mine, half_other = 128 * (xi % 2), 128 * (1 - xi % 2)
     heads = []
-    for start, size in ((0, 112), (112, 112)):
-        mine = head_rows(m, start, size)
+    for j in range(4):
+        mine = head_rows(m, half_mine + 32 * j, 32)
         heads.append(Send(mine, mine, to_back))
     near_head = Send(head_rows(m, 0, 256), head_rows(m, 0, 256), to_sib)
     q1.wait_recv()
@@ -137,8 +142,14 @@
         Send(p_ref.at[rows(256, 1 - core)], xh.at[:, feature], to_sib),
     ]
     xh[:, feature] = p_ref[rows(256, core)]
-    mine = head_rows(m, 224, 32)
-    heads.append(Send(mine, mine, to_opp))
+    side_heads, far_heads = [], []
+
+    def pass_head(j):
+        heads[j].wait_recv()
+        theirs = head_rows(opp, half_mine + 32 * j, 32)
+        side_heads.append(Send(theirs, theirs, at_x(1 if j % 2 == 0 else 3)))
+        far_heads.append(Send(theirs, theirs, to_sib))
+
 
     def own_lanes(value):
         quarters = [value[:, k * QM : (k + 1) * QM] for k in range(4)]
@@ -167,6 +178,8 @@
         norm = jnp.sqrt(jnp.sum(projected * projected, axis=1, keepdims=True) + EPS)
         return projected / norm, norm
 
+    pass_head(0)
+    pass_head(1)
     q0.wait_recv()
     q2.wait_recv()
     unit, norm = normalise(
@@ -175,13 +188,29 @@
     unit_q[...] = unit
     norm_q[...] = norm
     qb[2 * QM : 3 * QM] = unit.astype(BF)
+    def query_piece(k, h):
+        return qb.at[(2 - k) * QM + h * 32 : (2 - k) * QM + (h + 1) * 32]
+
     queries, auxes = [], []
+    for h in range(2):
+        for k in (1, -1):
+            queries.append(near_slab(query_piece(0, h), query_piece(k, h), k))
     for k in (1, -1, 2, -2):
-        queries.append(
-            near_slab(qb.at[2 * QM : 3 * QM], qb.at[(2 - k) * QM : (3 - k) * QM], k)
-        )
         auxes.append(near_slab(auxs.at[2 + k], auxr.at[2 - k], k))
 
+    def pass_on(h):
+        for i, k in enumerate((1, -1)):
+            queries[2 * h + i].wait_recv()
+            further.append(
+                Send(
+                    query_piece(k, h), query_piece(2 * k, h), at_slab(k),
+                    jnp.logical_and(inside(k), inside(-k)), inside(-2 * k),
+                )
+            )
+
+    further = []
+    pass_head(2)
+    pass_head(3)
     wide_q = [
         Send(q_ref.at[rows(QM, member)], xo.at[first : first + QM, rows(256, low)], to_opp)
         for first, member in ((0, opp), (192, osib))
@@ -194,11 +223,12 @@
     wide[2].wait_recv()
     near_head.wait_recv()
     projected = chip_part(low)
-    far_heads = []
-    for copy, (start, size) in ((heads[0], (0, 112)), (heads[2], (224, 32)), (heads[1], (112, 112))):
-        copy.wait_recv()
-        theirs = head_rows(opp, start, size)
+    for j in range(4):
+        side_heads[j].wait_recv()
+        theirs = head_rows(opp, half_other + 32 * j, 32)
         far_heads.append(Send(theirs, theirs, to_sib))
+        if j % 2 == 1:
+            pass_on(j // 2)
     for copy in wide[:2] + far_heads:
         copy.wait_recv()
     unit, norm = normalise(projected + chip_part(1 - low))
@@ -212,7 +242,7 @@
         Send(xh.at[rows(PM, low), rows(256, osib)], xo.at[192 + QM : 384, rows(256, 1 - low)], to_sib)
     )
     near.wait_recv()
-    for copy in queries + auxes:
+    for copy in further + auxes:
         copy.wait_recv()
 
     auxr[2] = auxs[2]
@@ -408,26 +438,17 @@
         fourth.append(Send(gz.at[rows(32, zi)], gz.at[rows(32, zi)], at_z(k)))
     for copy in fourth:
         copy.wait_recv()
-    upper = cols(128, 2 * xi + high)
-    lower = cols(128, 4 * high + xi)
-    oh_ref[0:128, upper] = gz[0:128]
-    oh_ref[128:256, lower] = gz[128:256]
-    mine = oh_ref.at[0:128, upper]
-    fifth = [Send(mine, mine, to_high)]
-    mine = oh_ref.at[128:256, lower]
-    for k in (2, 1, 3):
-        fifth.append(Send(mine, mine, at_x(k)))
-    fifth[0].wait_recv()
-    last = []
-    mine = oh_ref.at[0:128, cols(256, xi)]
-    for k in (2, 1, 3):
-        last.append(Send(mine, mine, at_x(k)))
-    for copy in fifth[1:]:
-        copy.wait_recv()
-    mine = oh_ref.at[128:256, cols(512, high)]
-    last.append(Send(mine, mine, to_high))
+    own = high * 4 + xi
+    last = [Send(gz, ga.at[own], at_high_x(k)) for k in (2, 1, 3)]
+    last += [Send(gz, ga.at[own], at_x(k)) for k in (2, 1, 3)]
+    last.append(Send(gz, ga.at[own], to_high))
+    ga[own] = gz[...]
     for copy in outs + last:
         copy.wait_recv()
+    for j in range(8):
+        upper, lower = 2 * (j % 4) + j // 4, j
+        oh_ref[0:128, upper * 128 : (upper + 1) * 128] = ga[j, 0:128]
+        oh_ref[128:256, lower * 128 : (lower + 1) * 128] = ga[j, 128:256]
     for copy in sent:
         copy.wait_send()
 
@@ -466,7 +487,7 @@
             half(3, 2, 128, 256), half(3, 128, 512),
             full(2, 128, 256), full(128, 512), half(2, 128, 256), half(128, 512),
             half(3, 128, 128), half(3, 128, 128), full(256, 128), half(256, 128),
-            half(7, 32, 128), half(256, 128),
+            half(7, 32, 128), half(256, 128), half(8, 256, 128),
             pltpu.SemaphoreType.DMA((7,)),
             pltpu.SemaphoreType.DMA((SEMS,)), pltpu.SemaphoreType.DMA((SEMS,)),
         ],

time: 85.9 us -> 81.2 us (0.945)
  Pallas kernels: 82.3 us -> 78 us
    pallas_call x1, Pallas kernels: 82.3 us -> 78 us  [body(): pl.pallas_call(kernel, out_shape=(jax.ShapeDtypeStruct((256, 256), BF), j...]
where the time goes in v4:
time: 81.2 us; the launch traced here: 81.1 us
  Pallas kernels  78 us (96%)
  local copies, waits for them, and re-layouts  1.36 us (2%)
  other arithmetic  1.09 us (1%)
    pallas_call x1, Pallas kernels, body(): pl.pallas_call(kernel, out_shape=(jax.ShapeDtypeStruct((256, 256), BF), j...  78 us

profile of v4, /device:TPU:8, one launch (start us, length us, event | category | flops | bytes accessed | tf_op | source)
XLA Modules:
  0.0 81.1 jit_solution(16188293014922758097)
XLA Ops:
  0.6 78.0 %shard_map.94 = (bf16[256,256]{1,0:T(8,128)(2,1)S(1)}, bf16[512,256]{1,0:T(8,128)(2,1)S(1)}, bf16[256,1024]{1,0:T(8,128)(2,1)S(1)}) custom-call(bf16[256,256]{1,0:T(8,128)(2,1)} %q_hbm.1, bf16[512,256]{1,0:T(8,128)(2,1)} %p_hbm.1, bf16[256,1024]{1,0:T(8,128)(2,1)} %head_hbm.1, s32[5,4,256]{2,1,0:T(4,128)} %bitcast.3, s32[64]{0:T(128)} %counts_hbm.1, ...), custom_call_target="tpu_custom_call" | custom-call | flops 3221225472 | bytes 4194304 | tf_op jit(solution)/shard_map/pallas_call | solution.py:466
  78.6 1.1 %convert_element_type.3 = f32[256,1024]{1,0:T(8,128)} convert(bf16[256,1024]{1,0:T(8,128)(2,1)S(1)} %get-tuple-element.8) | non-fusion elementwise | flops 262144 | bytes 1572864 | tf_op jit(solution)/shard_map/convert_element_type | solution.py:505
  79.7 0.7 copy.12
  80.4 0.7 copy.13

commit v5 on v4

--- a/solution.py
+++ b/solution.py
@@ -11,7 +11,7 @@
 QM = 64
 PM = 128
 NQ = 5 * QM
-SEMS = 128
+SEMS = 176
 MESH = pl.DeviceIdType.MESH
 BF = jnp.bfloat16
 F32 = jnp.float32
@@ -344,11 +344,16 @@
         own_terms = own_terms + gr[k].astype(F32)
     pgt[0:QM] = tangent(unit_q[...], norm_q[...], own_terms * scale - chosen * drop)
     shared = [Send(pgt.at[0:QM], pgt.at[192 : 192 + QM], to_sib)]
-    for copy in [p0] + p2:
-        copy.wait_recv()
-    summed = own_part + pr[0].astype(F32) + pz[...].astype(F32)
-    pgt[QM:192] = tangent(unit_p[rows(PM, low)], norm_p[rows(PM, low)], summed)
-    shared.append(Send(pgt.at[QM:192], pgt.at[192 + QM : 384], to_sib))
+    p0.wait_recv()
+    for i, piece in enumerate(pieces):
+        p2[i].wait_recv()
+        there = slice(QM + 64 * i, QM + 64 * (i + 1))
+        line = pl.ds(pl.multiple_of(PM * low + 64 * i, 64), 64)
+        summed = own_part[piece] + pr[0, piece].astype(F32) + pz[piece].astype(F32)
+        pgt[there] = tangent(unit_p[line], norm_p[line], summed)
+        shared.append(
+            Send(pgt.at[there], pgt.at[192 + QM + 64 * i : 192 + QM + 64 * (i + 1)], to_sib)
+        )
 
     def cols(size, index):
         return pl.ds(pl.multiple_of(index * size, size), size)
@@ -356,25 +361,35 @@
     for copy in wide_q + shared:
         copy.wait_recv()
 
-    first = []
-    for half in range(2):
+    first, second, third, fourth, last = ([[], []] for _ in range(5))
+
+    def term(half):
+        features = jnp.concatenate(
+            [xo[:, k + half * 128 : k + (half + 1) * 128] for k in (0, 256)], axis=1
+        )
+        total = lax.dot_general(
+            features, pgt[...], (((0,), (0,)), ((), ())), preferred_element_type=F32
+        )
         there = slice(half * 128, (half + 1) * 128)
         for block in range(2):
-            features = slice(block * 256 + half * 128, block * 256 + (half + 1) * 128)
-            total = lax.dot_general(
-                xo[:, features], pgt[...], (((0,), (0,)), ((), ())), preferred_element_type=F32
+            hf[block, there] = total[block * 128 : (block + 1) * 128]
+            hb[block, there] = total[block * 128 : (block + 1) * 128].astype(BF)
+
+    term(0)
+    for s in range(2):
+        there = slice(64 * s, 64 * (s + 1))
+        for k in (2, 1, 3):
+            first[s].append(
+                Send(hb.at[:, there, cols(256, (xi + k) % 4)], ax.at[s, k - 1], at_x(k))
             )
-            hf[block, there] = total
-            hb[block, there] = total.astype(BF)
-        if half == 0:
-            for k in (2, 1, 3):
-                first.append(
-                    Send(hb.at[:, there, cols(256, (xi + k) % 4)], ax.at[k - 1], at_x(k))
-                )
-        else:
-            first.append(Send(hb.at[low, there, cols(512, 1 - high)], cy.at[2], to_high))
-            first.append(Send(hb.at[1 - low, there, cols(512, high)], cy.at[0], to_opp))
-            first.append(Send(hb.at[1 - low, there, cols(512, 1 - high)], cy.at[1], to_back))
+    term(1)
+    for s in range(2):
+        there = slice(128 + 64 * s, 128 + 64 * (s + 1))
+        first[s] += [
+            Send(hb.at[low, there, cols(512, 1 - high)], cy.at[s, 2], to_high),
+            Send(hb.at[1 - low, there, cols(512, high)], cy.at[s, 0], to_opp),
+            Send(hb.at[1 - low, there, cols(512, 1 - high)], cy.at[s, 1], to_back),
+        ]
 
     eo[...] = lax.dot_general(
         pgt[0:192], head[...], (((1,), (1,)), ((), ())), preferred_element_type=F32
@@ -390,67 +405,100 @@
 
     outs = spread(sib, to_sib)
 
-    for copy in first[:3]:
-        copy.wait_recv()
-    total = hf[:, 0:128, cols(256, xi)]
-    for k in range(3):
-        total = total + ax[k].astype(F32)
-    a1f[...] = total
-    a1[...] = total.astype(BF)
-    second = [
-        Send(a1.at[low, :, cols(128, 1 - high)], ay.at[2], to_high),
-        Send(a1.at[1 - low, :, cols(128, high)], ay.at[0], to_opp),
-        Send(a1.at[1 - low, :, cols(128, 1 - high)], ay.at[1], to_back),
-    ]
-    for copy in first[3:]:
-        copy.wait_recv()
-    total = hf[low, 128:256, cols(512, high)]
-    for k in range(3):
-        total = total + cy[k].astype(F32)
-    c1f[...] = total
-    c1[...] = total.astype(BF)
-    for k in (2, 1, 3):
-        second.append(Send(c1.at[:, cols(128, (xi + k) % 4)], cx.at[k - 1], at_x(k)))
-    for copy in second:
-        copy.wait_recv()
-    total = a1f[low, :, cols(128, high)]
-    for k in range(3):
-        total = total + ay[k].astype(F32)
-    e1f[0:128] = total
-    e1[0:128] = total.astype(BF)
-    total = c1f[:, cols(128, xi)]
-    for k in range(3):
-        total = total + cx[k].astype(F32)
-    e1f[128:256] = total
-    e1[128:256] = total.astype(BF)
-    third = []
-    for k in (4, 3, 5, 2, 6, 1, 7):
-        third.append(Send(e1.at[rows(32, (zi + k) % 8)], ez.at[k - 1], at_z(k)))
+    def plus(total, ref, s, count):
+        for k in range(count):
+            total = total + ref[s, k].astype(F32)
+        return total
+
+    def along_second(s):
+        for copy in first[s][:3]:
+            copy.wait_recv()
+        total = plus(hf[:, 64 * s : 64 * (s + 1), cols(256, xi)], ax, s, 3)
+        a1f[s] = total
+        a1[s] = total.astype(BF)
+        second[s] += [
+            Send(a1.at[s, low, :, cols(128, 1 - high)], ay.at[s, 2], to_high),
+            Send(a1.at[s, 1 - low, :, cols(128, high)], ay.at[s, 0], to_opp),
+            Send(a1.at[s, 1 - low, :, cols(128, 1 - high)], ay.at[s, 1], to_back),
+        ]
+        for copy in first[s][3:]:
+            copy.wait_recv()
+        total = plus(hf[low, 128 + 64 * s : 128 + 64 * (s + 1), cols(512, high)], cy, s, 3)
+        c1f[s] = total
+        c1[s] = total.astype(BF)
+        for k in (2, 1, 3):
+            second[s].append(
+                Send(c1.at[s, :, cols(128, (xi + k) % 4)], cx.at[s, k - 1], at_x(k))
+            )
+
+    def along_z(s):
+        for copy in second[s]:
+            copy.wait_recv()
+        total = plus(a1f[s, low, :, cols(128, high)], ay, s, 3)
+        e1f[s, 0:64] = total
+        e1[s, 0:64] = total.astype(BF)
+        total = plus(c1f[s, :, cols(128, xi)], cx, s, 3)
+        e1f[s, 64:128] = total
+        e1[s, 64:128] = total.astype(BF)
+        for k in (4, 3, 5, 2, 6, 1, 7):
+            third[s].append(Send(e1.at[s, rows(16, (zi + k) % 8)], ez.at[s, k - 1], at_z(k)))
+
+    def back_z(s):
+        for copy in third[s]:
+            copy.wait_recv()
+        mine = gz.at[s, rows(16, zi)]
+        mine[...] = plus(e1f[s, rows(16, zi)], ez, s, 7).astype(BF)
+        for k in (4, 3, 5, 2, 6, 1, 7):
+            fourth[s].append(Send(mine, mine, at_z(k)))
+
+    own = high * 4 + xi
+
+    def back(s):
+        for copy in fourth[s]:
+            copy.wait_recv()
+        last[s] += [Send(gz.at[s], ga.at[s, own], at_high_x(k)) for k in (2, 1, 3)]
+        last[s] += [Send(gz.at[s], ga.at[s, own], at_x(k)) for k in (2, 1, 3)]
+        last[s].append(Send(gz.at[s], ga.at[s, own], to_high))
+        ga[s, own] = gz[s]
+
+    along_second(0)
+    along_second(1)
+    along_z(0)
+    along_z(1)
     outs += spread(opp, to_opp) + spread(osib, to_osib)
-    for copy in third:
-        copy.wait_recv()
-    total = e1f[rows(32, zi)]
-    for k in range(7):
-        total = total + ez[k].astype(F32)
-    gz[rows(32, zi)] = total.astype(BF)
-    fourth = []
-    for k in (4, 3, 5, 2, 6, 1, 7):
-        fourth.append(Send(gz.at[rows(32, zi)], gz.at[rows(32, zi)], at_z(k)))
-    for copy in fourth:
-        copy.wait_recv()
-    own = high * 4 + xi
-    last = [Send(gz, ga.at[own], at_high_x(k)) for k in (2, 1, 3)]
-    last += [Send(gz, ga.at[own], at_x(k)) for k in (2, 1, 3)]
-    last.append(Send(gz, ga.at[own], to_high))
-    ga[own] = gz[...]
-    for copy in outs + last:
-        copy.wait_recv()
-    for j in range(8):
-        upper, lower = 2 * (j % 4) + j // 4, j
-        oh_ref[0:128, upper * 128 : (upper + 1) * 128] = ga[j, 0:128]
-        oh_ref[128:256, lower * 128 : (lower + 1) * 128] = ga[j, 128:256]
+    back_z(0)
+    back_z(1)
+    back(0)
+    back(1)
+    for s in range(2):
+        for copy in last[s]:
+            copy.wait_recv()
+        for j in range(8):
+            upper, lower = 128 * (2 * (j % 4) + j // 4), 128 * j
+            oh_ref[64 * s : 64 * (s + 1), upper : upper + 128] = ga[s, j, 0:64]
+            oh_ref[128 + 64 * s : 128 + 64 * (s + 1), lower : lower + 128] = ga[s, j, 64:128]
+    for copy in outs:
+        copy.wait_recv()
     for copy in sent:
         copy.wait_send()
+
+
+def emit(query, passage, term, query_out, passage_out, head_out, wide, sems):
+    copies = [
+        pltpu.make_async_copy(query, query_out, sems.at[0]),
+        pltpu.make_async_copy(passage, passage_out, sems.at[1]),
+    ]
+    for copy in copies:
+        copy.start()
+    for part in range(2):
+        there = slice(part * 128, (part + 1) * 128)
+        wide[there] = term[there].astype(F32)
+        copies.append(
+            pltpu.make_async_copy(wide.at[there], head_out.at[there], sems.at[2 + part])
+        )
+        copies[-1].start()
+    for copy in copies:
+        copy.wait()
 
 
 def body(query_emb, passage_emb, head, fn_mask, counts, positive_slot, query_weight):
@@ -463,7 +511,7 @@
     def full(*shape):
         return pltpu.VMEM(shape, F32)
 
-    query_grad, passage_grad, head_grad = pl.pallas_call(
+    grads = pl.pallas_call(
         kernel,
         out_shape=(
             jax.ShapeDtypeStruct((256, 256), BF),
@@ -484,10 +532,10 @@
             half(2, PM, D), half(2, PM, D), half(PM, D), half(PM, D),
             half(384, 512), half(384, D), half(192, D),
             full(2, 256, D), half(2, 256, D),
-            half(3, 2, 128, 256), half(3, 128, 512),
-            full(2, 128, 256), full(128, 512), half(2, 128, 256), half(128, 512),
-            half(3, 128, 128), half(3, 128, 128), full(256, 128), half(256, 128),
-            half(7, 32, 128), half(256, 128), half(8, 256, 128),
+            half(2, 3, 2, 64, 256), half(2, 3, 64, 512),
+            full(2, 2, 64, 256), full(2, 64, 512), half(2, 2, 64, 256), half(2, 64, 512),
+            half(2, 3, 64, 128), half(2, 3, 64, 128), full(2, 128, 128), half(2, 128, 128),
+            half(2, 7, 16, 128), half(2, 128, 128), half(2, 8, 128, 128),
             pltpu.SemaphoreType.DMA((7,)),
             pltpu.SemaphoreType.DMA((SEMS,)), pltpu.SemaphoreType.DMA((SEMS,)),
         ],
@@ -502,7 +550,18 @@
             positive_slot.reshape(1, -1), query_weight.reshape(1, -1),
         )
     ])
-    return query_grad, passage_grad, head_grad.astype(F32)
+    return pl.pallas_call(
+        emit,
+        out_shape=(
+            jax.ShapeDtypeStruct((256, 256), BF),
+            jax.ShapeDtypeStruct((512, 256), BF),
+            jax.ShapeDtypeStruct((256, D), F32),
+        ),
+        in_specs=[vmem] * 3,
+        out_specs=(hbm,) * 3,
+        scratch_shapes=[full(256, D), pltpu.SemaphoreType.DMA((4,))],
+        compiler_params=pltpu.CompilerParams(vmem_limit_bytes=8 << 20),
+    )(*grads)
 
 
 def solution(mesh):

time: 81.2 us -> 78.8 us (0.970)
  local copies, waits for them, and re-layouts: 1.36 us -> 0 us
  other arithmetic: 1.09 us -> 0 us
    unnamed x2 -> x0, local copies, waits for them, and re-layouts: 1.36 us -> none
    pallas_call x0 -> x1, Pallas kernels: none -> 1.13 us  [body(): pl.pallas_call(emit, out_shape=(jax.ShapeDtypeStruct((256, 256), BF), jax...]
    convert_element_type x1 -> x0, other arithmetic: 1.09 us -> none  [body(): return (query_grad, passage_grad, head_grad.astype(F32))]
    pallas_call x1, Pallas kernels: 78 us -> 77 us  [body(): pl.pallas_call(kernel, out_shape=(jax.ShapeDtypeStruct((256, 256), BF), j...]
where the time goes in v5:
time: 78.8 us; the launch traced here: 78.7 us
  Pallas kernels  78.1 us (99%)
    pallas_call x1, Pallas kernels, body(): pl.pallas_call(kernel, out_shape=(jax.ShapeDtypeStruct((256, 256), BF), j...  77 us

profile of v5, /device:TPU:8, one launch (start us, length us, event | category | flops | bytes accessed | tf_op | source)
XLA Modules:
  0.0 78.7 jit_solution(4180815005238806391)
XLA Ops:
  0.6 77.0 %shard_map.94 = (bf16[256,256]{1,0:T(8,128)(2,1)S(1)}, bf16[512,256]{1,0:T(8,128)(2,1)S(1)}, bf16[256,1024]{1,0:T(8,128)(2,1)S(1)}) custom-call(bf16[256,256]{1,0:T(8,128)(2,1)} %q_hbm.1, bf16[512,256]{1,0:T(8,128)(2,1)} %p_hbm.1, bf16[256,1024]{1,0:T(8,128)(2,1)} %head_hbm.1, s32[5,4,256]{2,1,0:T(4,128)} %bitcast.3, s32[64]{0:T(128)} %counts_hbm.1, ...), custom_call_target="tpu_custom_call" | custom-call | flops 3221225472 | bytes 4194304 | tf_op jit(solution)/shard_map/pallas_call | solution.py:514
  77.6 1.1 %shard_map.95 = (bf16[256,256]{1,0:T(8,128)(2,1)}, bf16[512,256]{1,0:T(8,128)(2,1)}, f32[256,1024]{1,0:T(8,128)}) custom-call(bf16[256,256]{1,0:T(8,128)(2,1)S(1)} %get-tuple-element.6.query, bf16[512,256]{1,0:T(8,128)(2,1)S(1)} %get-tuple-element.7.passage, bf16[256,1024]{1,0:T(8,128)(2,1)S(1)} %get-tuple-element.8.term), custom_call_target="tpu_custom_call" | custom-call | tf_op jit(solution)/shard_map/pallas_call | solution.py:553

commit v6 on v5

--- a/solution.py
+++ b/solution.py
@@ -90,9 +90,6 @@
     def rows(count, index):
         return pl.ds(pl.multiple_of(count * index, count), count)
 
-    barrier = pltpu.get_barrier_semaphore()
-    for peer in peers:
-        pl.semaphore_signal(barrier, inc=1, device_id=peer, device_id_type=MESH)
     loads = [
         pltpu.make_async_copy(src, dst, lsem.at[i])
         for i, (src, dst) in enumerate((
@@ -103,6 +100,9 @@
     ]
     for copy in loads:
         copy.start()
+    barrier = pltpu.get_barrier_semaphore()
+    for peer in peers:
+        pl.semaphore_signal(barrier, inc=1, device_id=peer, device_id_type=MESH)
 
     for k in (-4, -3, -2, -1, 1, 2, 3, 4):
         @pl.when(jnp.logical_not(inside(k)))
@@ -110,8 +110,14 @@
             ttr[k + 4] = jnp.zeros((4, 128), F32)
             if abs(k) <= 2:
                 qb[(2 + k) * QM : (3 + k) * QM] = jnp.zeros((QM, D), BF)
-                gr[k + 2] = jnp.zeros((QM, D), BF)
+                if abs(k) == 1:
+                    gr[k + 2] = jnp.zeros((QM, D), BF)
                 auxr[k + 2] = jnp.zeros((8, 128), F32)
+
+    for k in (1, -1):
+        @pl.when(jnp.logical_not(jnp.logical_and(inside(k), inside(-k))))
+        def _():
+            gr[2 - 2 * k] = jnp.zeros((QM, D), BF)
 
     loads[0].wait()
     loads[1].wait()
@@ -188,6 +194,8 @@
     unit_q[...] = unit
     norm_q[...] = norm
     qb[2 * QM : 3 * QM] = unit.astype(BF)
+    halves = [slice(0, 32), slice(32, 64)]
+
     def query_piece(k, h):
         return qb.at[(2 - k) * QM + h * 32 : (2 - k) * QM + (h + 1) * 32]
 
@@ -277,11 +285,32 @@
     terms = lax.dot_general(
         eb[...], pb[...], (((0,), (0,)), ((), ())), preferred_element_type=F32
     )
+    relay = []
+    for h in range(2):
+        for k in (1, -1):
+            lines = slice((2 + 2 * k) * QM + 32 * h, (2 + 2 * k) * QM + 32 * (h + 1))
+            gs[2 + 2 * k, halves[h]] = terms[lines].astype(BF)
+            relay.append(
+                Send(
+                    gs.at[2 + 2 * k, halves[h]], gr.at[2 - 2 * k, halves[h]], at_slab(k),
+                    jnp.logical_and(inside(k), inside(2 * k)),
+                    jnp.logical_and(inside(k), inside(-k)),
+                )
+            )
+    own_terms = terms[2 * QM : 3 * QM]
+    nearest = {k: terms[(2 + k) * QM : (3 + k) * QM] for k in (1, -1)}
     returns = []
-    for k in (2, -2, 1, -1):
-        gs[2 + k] = terms[(2 + k) * QM : (3 + k) * QM].astype(BF)
-        returns.append(near_slab(gs.at[2 + k], gr.at[2 - k], k))
-    own_terms = terms[2 * QM : 3 * QM]
+
+    def add_relayed(h):
+        for i, k in enumerate((1, -1)):
+            relay[2 * h + i].wait_recv()
+            gs[2 + k, halves[h]] = (
+                nearest[k][halves[h]] + gr[2 - 2 * k, halves[h]].astype(F32)
+            ).astype(BF)
+            returns.append(
+                near_slab(gs.at[2 + k, halves[h]], gr.at[2 - k, halves[h]], k)
+            )
+
 
     ttr[4] = tts[...]
     for copy in totals:
@@ -310,11 +339,13 @@
     pieces = [slice(0, 64), slice(64, 128)]
     p1 = [Send(pps.at[1, piece], pr.at[1, piece], to_sib) for piece in pieces]
     part = passage_terms(p_opp)
+    add_relayed(0)
     p2 = []
     for copy, piece in zip(p1, pieces):
         copy.wait_recv()
         py[piece] = (part[piece] + pr[1, piece].astype(F32)).astype(BF)
         p2.append(Send(py.at[piece], pz.at[piece], to_opp))
+    add_relayed(1)
     pps[0] = passage_terms(p_sib).astype(BF)
     p0 = Send(pps.at[0], pr.at[0], to_sib)
     own_part = passage_terms(p_own)
@@ -340,7 +371,7 @@
     drop = column(weight * own_rest / (own_whole * TAU))
     for copy in returns:
         copy.wait_recv()
-    for k in (0, 1, 3, 4):
+    for k in (1, 3):
         own_terms = own_terms + gr[k].astype(F32)
     pgt[0:QM] = tangent(unit_q[...], norm_q[...], own_terms * scale - chosen * drop)
     shared = [Send(pgt.at[0:QM], pgt.at[192 : 192 + QM], to_sib)]

time: 78.8 us -> 77.8 us (0.987)
  Pallas kernels: 78.1 us -> 76.8 us
    pallas_call x1, Pallas kernels: 77 us -> 75.7 us  [body(): pl.pallas_call(kernel, out_shape=(jax.ShapeDtypeStruct((256, 256), BF), j...]
where the time goes in v6:
time: 77.8 us; the launch traced here: 77.5 us
  Pallas kernels  76.8 us (99%)
    pallas_call x1, Pallas kernels, body(): pl.pallas_call(kernel, out_shape=(jax.ShapeDtypeStruct((256, 256), BF), j...  75.7 us

profile of v6, /device:TPU:8, one launch (start us, length us, event | category | flops | bytes accessed | tf_op | source)
XLA Modules:
  0.0 77.5 jit_solution(6461907071660802163)
XLA Ops:
  0.6 75.7 %shard_map.94 = (bf16[256,256]{1,0:T(8,128)(2,1)S(1)}, bf16[512,256]{1,0:T(8,128)(2,1)S(1)}, bf16[256,1024]{1,0:T(8,128)(2,1)S(1)}) custom-call(bf16[256,256]{1,0:T(8,128)(2,1)} %q_hbm.1, bf16[512,256]{1,0:T(8,128)(2,1)} %p_hbm.1, bf16[256,1024]{1,0:T(8,128)(2,1)} %head_hbm.1, s32[5,4,256]{2,1,0:T(4,128)} %bitcast.3, s32[64]{0:T(128)} %counts_hbm.1, ...), custom_call_target="tpu_custom_call" | custom-call | flops 3221225472 | bytes 4194304 | tf_op jit(solution)/shard_map/pallas_call | solution.py:545
  76.3 1.1 %shard_map.95 = (bf16[256,256]{1,0:T(8,128)(2,1)}, bf16[512,256]{1,0:T(8,128)(2,1)}, f32[256,1024]{1,0:T(8,128)}) custom-call(bf16[256,256]{1,0:T(8,128)(2,1)S(1)} %get-tuple-element.6.query, bf16[512,256]{1,0:T(8,128)(2,1)S(1)} %get-tuple-element.7.passage, bf16[256,1024]{1,0:T(8,128)(2,1)S(1)} %get-tuple-element.8.term), custom_call_target="tpu_custom_call" | custom-call | tf_op jit(solution)/shard_map/pallas_call | solution.py:584

commit v7 on v6

--- a/solution.py
+++ b/solution.py
@@ -330,15 +330,20 @@
         else:
             auxc[7:8, lanes] = jnp.zeros((1, QM), F32)
 
-    def passage_terms(index):
+    def coefficients(index):
         is_positive = (slot_ids + index * PM).astype(F32) == auxc[5:6, :]
-        coefficient = jnp.where(is_positive, -auxc[7:8, :], ef[rows(PM, index)] * auxc[6:7, :])
-        return jnp.dot(coefficient.astype(BF), qb[...], preferred_element_type=F32)
-
-    pps[1] = passage_terms(p_osib).astype(BF)
+        value = jnp.where(is_positive, -auxc[7:8, :], ef[rows(PM, index)] * auxc[6:7, :])
+        return value.astype(BF)
+
+    def passage_terms(*indices):
+        value = jnp.concatenate([coefficients(index) for index in indices], axis=0)
+        return jnp.dot(value, qb[...], preferred_element_type=F32)
+
+    both = passage_terms(p_osib, p_opp)
+    pps[1] = both[0:PM].astype(BF)
     pieces = [slice(0, 64), slice(64, 128)]
     p1 = [Send(pps.at[1, piece], pr.at[1, piece], to_sib) for piece in pieces]
-    part = passage_terms(p_opp)
+    part = both[PM:]
     add_relayed(0)
     p2 = []
     for copy, piece in zip(p1, pieces):
@@ -346,9 +351,10 @@
         py[piece] = (part[piece] + pr[1, piece].astype(F32)).astype(BF)
         p2.append(Send(py.at[piece], pz.at[piece], to_opp))
     add_relayed(1)
-    pps[0] = passage_terms(p_sib).astype(BF)
+    both = passage_terms(p_sib, p_own)
+    pps[0] = both[0:PM].astype(BF)
     p0 = Send(pps.at[0], pr.at[0], to_sib)
-    own_part = passage_terms(p_own)
+    own_part = both[PM:]
 
     def tangent(unit, norm, grad):
         radial = jnp.sum(unit * grad, axis=1, keepdims=True)

time: 77.8 us -> 77.6 us (level)
  no operation moved by 1% of the time
where the time goes in v7:
time: 77.6 us; the launch traced here: 77.5 us
  Pallas kernels  76.9 us (99%)
    pallas_call x1, Pallas kernels, body(): pl.pallas_call(kernel, out_shape=(jax.ShapeDtypeStruct((256, 256), BF), j...  75.8 us

profile of v7, /device:TPU:8, one launch (start us, length us, event | category | flops | bytes accessed | tf_op | source)
XLA Modules:
  0.0 77.5 jit_solution(7815790972236283345)
XLA Ops:
  0.6 75.8 %shard_map.94 = (bf16[256,256]{1,0:T(8,128)(2,1)S(1)}, bf16[512,256]{1,0:T(8,128)(2,1)S(1)}, bf16[256,1024]{1,0:T(8,128)(2,1)S(1)}) custom-call(bf16[256,256]{1,0:T(8,128)(2,1)} %q_hbm.1, bf16[512,256]{1,0:T(8,128)(2,1)} %p_hbm.1, bf16[256,1024]{1,0:T(8,128)(2,1)} %head_hbm.1, s32[5,4,256]{2,1,0:T(4,128)} %bitcast.3, s32[64]{0:T(128)} %counts_hbm.1, ...), custom_call_target="tpu_custom_call" | custom-call | flops 3221225472 | bytes 4194304 | tf_op jit(solution)/shard_map/pallas_call | solution.py:551
  76.4 1.1 %shard_map.95 = (bf16[256,256]{1,0:T(8,128)(2,1)}, bf16[512,256]{1,0:T(8,128)(2,1)}, f32[256,1024]{1,0:T(8,128)}) custom-call(bf16[256,256]{1,0:T(8,128)(2,1)S(1)} %get-tuple-element.6.query, bf16[512,256]{1,0:T(8,128)(2,1)S(1)} %get-tuple-element.7.passage, bf16[256,1024]{1,0:T(8,128)(2,1)S(1)} %get-tuple-element.8.term), custom_call_target="tpu_custom_call" | custom-call | tf_op jit(solution)/shard_map/pallas_call | solution.py:590
